TPU v7x, 32 devices: a whole 2x2x4 slice. The times are simulated.
32 devices in a mesh: wide: 8 (over z, x), narrow: 4 (over y, core).
Axes of the slice: x: 2, y: 2, z: 4, core: 2. Of those that a mesh axis runs over, the one named last changes fastest.
Arguments:
- hidden_in: float32 [8192, 768], P(('wide', 'narrow')), may hold values from -6 to 6
- out_cot: float32 [8192, 768], P(('wide', 'narrow')), may hold values from -6 to 6
- lengths: int32 [8], P('wide'), may hold values from 1 to 1024, as said below
- norm_gain: float32 [768], P('narrow'), may hold values from 0.5 to 1.5
- w_zx: float32 [2, 768, 1536], P(None, 'wide', 'narrow'), may hold values from -0.21875 to 0.21875
- w_bc: float32 [768, 256], P('wide'), may hold values from -0.21875 to 0.21875
- w_dt: float32 [768, 24, 2], P('wide', 'narrow'), may hold values from -0.109375 to 0.109375
- conv_x: float32 [4, 1536], P(None, 'narrow'), may hold values from -0.5 to 0.5
- conv_bc: float32 [4, 256], replicated, may hold values from -0.5 to 0.5
- head_params: float32 [5, 24], P(None, 'narrow'), as said below
- out_gain: float32 [1536], P('narrow'), as said below
- w_out: float32 [1536, 768], P('narrow', 'wide'), may hold values from -0.15625 to 0.15625
- left_statistic_gate: float32 [2, 4, 768, 768], P(None, 'narrow', 'wide')
- stat_right_zx: float32 [2, 1536, 384], P(None, 'narrow'), as said below
- stat_left_out: float32 [1536, 384], P('narrow'), as said below
- stat_right_out: float32 [4, 768, 768], P('narrow', 'wide')
- inverse_root_left_gate: float32 [2, 4, 768, 768], P(None, 'narrow', 'wide')
- inverse_root_right_gate: float32 [2, 1536, 384], P(None, 'narrow'), as said below
- root_left_out: float32 [1536, 384], P('narrow'), as said below
- root_right_out: float32 [4, 768, 768], P('narrow', 'wide')
Outputs:
- block_out: float32 [8192, 768], P(('wide', 'narrow'))
- in_grad: float32 [8192, 768], P(('wide', 'narrow'))
- clip_norm: float32 [], replicated
- grad_zx: float32 [2, 768, 1536], P(None, 'wide', 'narrow')
- new_w_zx: float32 [2, 768, 1536], P(None, 'wide', 'narrow')
- new_stat_left_zx: float32 [2, 4, 768, 768], P(None, 'narrow', 'wide')
- new_stat_right_zx: float32 [2, 1536, 384], P(None, 'narrow')
- grad_out: float32 [1536, 768], P('narrow', 'wide')
- new_w_out: float32 [1536, 768], P('narrow', 'wide')
- new_stat_left_out: float32 [1536, 384], P('narrow')
- new_stat_right_out: float32 [4, 768, 768], P('narrow', 'wide')
- grad_bc: float32 [768, 256], P('wide')
- new_w_bc: float32 [768, 256], P('wide')
- grad_dt: float32 [768, 24, 2], P('wide', 'narrow')
- new_w_dt: float32 [768, 24, 2], P('wide', 'narrow')
- grad_conv_x: float32 [4, 1536], P(None, 'narrow')
- new_conv_x: float32 [4, 1536], P(None, 'narrow')
- grad_conv_bc: float32 [4, 256], replicated
- new_conv_bc: float32 [4, 256], replicated
- grad_head: float32 [5, 24], P(None, 'narrow')
- new_head: float32 [5, 24], P(None, 'narrow')
- grad_out_gain: float32 [1536], P('narrow')
- new_out_gain: float32 [1536], P('narrow')
- grad_norm_gain: float32 [768], P('narrow')
- new_norm_gain: float32 [768], P('narrow')
Inputs may be any that keep to these rules, and one draw needn't show every extreme that they name: `lengths`: real tokens of each sequence; the remaining slots of its 1024 are padding. `head_params`: per head: the first two rows are step biases, the next two log rates, the last the diagonal term. `out_gain`: positive gains. `stat_right_zx`: each 384 x 384 block is symmetric positive definite. `stat_left_out`: each 384 x 384 block is symmetric positive definite. `inverse_root_right_gate`: each 384 x 384 block is symmetric. `root_left_out`: each 384 x 384 block is symmetric.
All inputs are finite; a program needn't handle non-finite values.
Results may differ from a plain program's by a relative error of at most 0.0003.
Values sent between devices are 32-bit elements; how exact they have to be, the bound alone decides.
A program may use at most 192 MiB of HBM per device.

v0:
```python
import jax
import jax.numpy as jnp
from jax import lax
from jax.sharding import PartitionSpec as P

SPAN = 128


def silu(v):
    return v / (1.0 + jnp.exp(-v))


def causal(values, taps):
    count = taps.shape[0]
    length = values.shape[1]
    padded = jnp.pad(values, ((0, 0), (count - 1, 0), (0, 0)))
    total = taps[0] * padded[:, 0:length]
    for j in range(1, count):
        total = total + taps[j] * padded[:, j : j + length]
    return total


def scan_ssd(xh, steps, logs, bmat, cmat, span):
    hyper_parameters = lax.Precision.HIGHEST
    seqs, length, heads, width = xh.shape
    blocks = length // span
    xq = xh.reshape(seqs, blocks, span, heads, width).transpose(0, 1, 3, 2, 4)
    dq = steps.reshape(seqs, blocks, span, heads).transpose(0, 1, 3, 2)
    aq = logs.reshape(seqs, blocks, span, heads).transpose(0, 1, 3, 2)
    bq = bmat.reshape(seqs, blocks, span, -1)
    cq = cmat.reshape(seqs, blocks, span, -1)
    cum = jnp.cumsum(aq, axis=-1)
    lower = jnp.arange(span)[:, None] >= jnp.arange(span)[None, :]
    diff = cum[..., :, None] - cum[..., None, :]
    decay = jnp.where(lower, jnp.exp(jnp.where(lower, diff, 0.0)), 0.0)
    inner = jnp.einsum("sctn,scun->sctu", cq, bq, precision=hyper_parameters)
    weights = inner[:, :, None] * decay * dq[..., None, :]
    y_in = jnp.einsum("schtu,schup->schtp", weights, xq, precision=hyper_parameters)
    tail = jnp.exp(cum[..., -1:] - cum) * dq
    states = jnp.einsum("scun,schu,schup->schnp", bq, tail, xq, precision=hyper_parameters)
    totals = jnp.exp(cum[..., -1])

    def advance(carry, inputs):
        piece, factor = inputs
        return (carry * factor[..., None, None] + piece, carry)

    start = jnp.zeros((seqs, heads, bq.shape[-1], width), jnp.float32)
    _, before = lax.scan(
        jax.checkpoint(advance), start, (states.transpose(1, 0, 2, 3, 4), totals.transpose(1, 0, 2))
    )
    before = before.transpose(1, 0, 2, 3, 4)
    y_out = (
        jnp.einsum("sctn,schnp->schtp", cq, before, precision=hyper_parameters)
        * jnp.exp(cum)[..., None]
    )
    return (y_in + y_out).transpose(0, 1, 3, 2, 4).reshape(seqs, length, heads, width)


def mixer(normed, w_zx, w_bc, w_dt, conv_x, conv_bc, head_params, live, seqs):
    hyper_parameters = lax.Precision.HIGHEST
    tokens = normed.shape[0]
    seq_len = tokens // seqs
    heads = w_dt.shape[1]
    state = w_bc.shape[1] // 4
    gate = jnp.dot(normed, w_zx[0], precision=hyper_parameters)
    xin = jnp.dot(normed, w_zx[1], precision=hyper_parameters)
    bc_pre = jnp.dot(normed, w_bc, precision=hyper_parameters)
    dt_pre = jnp.dot(
        normed, w_dt.reshape(w_dt.shape[0], heads * 2), precision=hyper_parameters
    ).reshape(tokens, heads, 2)
    xconv = (
        silu(causal(xin.reshape(seqs, seq_len, -1), conv_x))
        * live.reshape(seqs, seq_len)[..., None]
    )
    bconv = silu(causal(bc_pre.reshape(seqs, seq_len, -1), conv_bc))
    steps = jax.nn.softplus(dt_pre + head_params[0:2].T)
    logs = -jnp.exp(head_params[2:4].T) * steps
    width = xconv.shape[-1] // heads
    xh = xconv.reshape(seqs, seq_len, heads, width)
    steps = steps.reshape(seqs, seq_len, heads, 2)
    logs = logs.reshape(seqs, seq_len, heads, 2)
    b_fwd = bconv[..., 0:state]
    c_fwd = bconv[..., state : 2 * state]
    b_rev = bconv[..., 2 * state : 3 * state]
    c_rev = bconv[..., 3 * state : 4 * state]
    forward = scan_ssd(xh, steps[..., 0], logs[..., 0], b_fwd, c_fwd, SPAN)
    backward = jnp.flip(
        scan_ssd(
            jnp.flip(xh, 1),
            jnp.flip(steps[..., 1], 1),
            jnp.flip(logs[..., 1], 1),
            jnp.flip(b_rev, 1),
            jnp.flip(c_rev, 1),
            SPAN,
        ),
        1,
    )
    fwd_part = jnp.pad(forward[:, :-1], ((0, 0), (1, 0), (0, 0), (0, 0)))
    rev_part = jnp.pad(backward[:, 1:], ((0, 0), (0, 1), (0, 0), (0, 0)))
    mixed = fwd_part + rev_part + head_params[4][:, None] * xh
    return mixed.reshape(tokens, -1) * silu(gate)


def square_sum(arrays):
    total = jnp.float32(0.0)
    for item in arrays:
        total = total + jnp.sum(item * item)
    return total


def local(
    hidden_in,
    out_cot,
    lengths,
    norm_gain,
    w_zx,
    w_bc,
    w_dt,
    conv_x,
    conv_bc,
    head_params,
    out_gain,
    w_out,
    left_statistic_gate,
    stat_right_zx,
    stat_left_out,
    stat_right_out,
    inverse_root_left_gate,
    inverse_root_right_gate,
    root_left_out,
    root_right_out,
):
    hyper_parameters = lax.Precision.HIGHEST
    wide_zx, wide_bc, wide_dt, wide_out = (
        lax.all_gather(w_zx, "wide", axis=1, tiled=True),
        lax.all_gather(w_bc, "wide", axis=0, tiled=True),
        lax.all_gather(w_dt, "wide", axis=0, tiled=True),
        lax.all_gather(w_out, "wide", axis=1, tiled=True),
    )
    full_in, full_gain = (
        lax.all_gather(hidden_in, "narrow", axis=0, tiled=True),
        lax.all_gather(norm_gain, "narrow", axis=0, tiled=True),
    )
    tokens = full_in.shape[0]
    width_model = full_in.shape[1]
    own_rows = hidden_in.shape[0]
    shard = norm_gain.shape[0]
    seq_dev = lengths.shape[0]
    seq_len = tokens // seq_dev
    narrow_id = lax.axis_index("narrow")
    row_start = narrow_id * own_rows
    live = (jnp.arange(seq_len)[None, :] < lengths[:, None]).astype(jnp.float32).reshape(-1)
    live_own = lax.dynamic_slice_in_dim(live, row_start, own_rows, 0)
    inv_rms = lax.rsqrt(jnp.mean(full_in * full_in, axis=-1) + 1e-05)
    normed = full_in * inv_rms[:, None] * full_gain

    def local_mix(n_in, a_in, b_in, c_in, d_in, e_in, f_in):
        return mixer(n_in, a_in, b_in, c_in, d_in, e_in, f_in, live, seq_dev)

    gated, gated_back = jax.vjp(
        local_mix, normed, wide_zx, wide_bc, wide_dt, conv_x, conv_bc, head_params
    )
    inner_total = gated.shape[1] * lax.axis_size("narrow")
    squares = lax.psum(jnp.sum(gated * gated, axis=1), "narrow")
    gate_rms = lax.rsqrt(squares / inner_total + 1e-05)
    onorm = gated * gate_rms[:, None] * out_gain
    partial_value = jnp.dot(onorm, wide_out, precision=hyper_parameters)
    branch = lax.psum_scatter(partial_value, "narrow", scatter_dimension=0, tiled=True)
    block_out = hidden_in + live_own[:, None] * branch
    dbranch = lax.all_gather(live_own[:, None] * out_cot, "narrow", axis=0, tiled=True)
    d_onorm = jnp.dot(dbranch, wide_out.T, precision=hyper_parameters)
    grad_out = jnp.dot(onorm.T, dbranch, precision=hyper_parameters)
    grad_ogain = jnp.sum(gated * gate_rms[:, None] * d_onorm, axis=0)
    scaled = d_onorm * out_gain
    inner_dot = lax.psum(jnp.sum(gated * scaled, axis=1), "narrow")
    dgated = gate_rms[:, None] * scaled - gated * (gate_rms**3 * inner_dot / inner_total)[:, None]
    d_normed, d_zx, d_bc, d_dt, d_convx, d_convbc, d_head = gated_back(dgated)
    dnormed = lax.psum(d_normed, "narrow")
    total_dot = jnp.sum(full_in * full_gain * dnormed, axis=1)
    dx_full = (
        inv_rms[:, None] * full_gain * dnormed
        - full_in * (inv_rms**3 * total_dot / width_model)[:, None]
    )
    dgain_full = jnp.sum(full_in * inv_rms[:, None] * dnormed, axis=0)
    dx_share = lax.dynamic_slice_in_dim(dx_full, row_start, own_rows, 0)
    grad_ngain = lax.dynamic_slice_in_dim(dgain_full, narrow_id * shard, shard, 0)
    in_grad = out_cot + dx_share
    g_zx, g_out, g_dt, g_cx, g_head, g_og, g_ng = lax.psum(
        (d_zx, grad_out, d_dt, d_convx, d_head, grad_ogain, grad_ngain), "wide"
    )
    g_bc, g_cbc = lax.psum((d_bc, d_convbc), ("wide", "narrow"))
    local_squares = square_sum((g_zx, g_out, g_dt, g_cx, g_head, g_og, g_ng))
    total_squares = lax.psum(local_squares, "narrow") + square_sum((g_bc, g_cbc))
    clip_norm = jnp.sqrt(total_squares)
    factor = 1.0 / jnp.maximum(clip_norm, 1.0)
    cotangent_gate_input = g_zx * factor
    c_out = g_out * factor
    c_bc = g_bc * factor
    c_dt = g_dt * factor
    c_cx = g_cx * factor
    c_cbc = g_cbc * factor
    c_head = g_head * factor
    c_og = g_og * factor
    c_ng = g_ng * factor
    wide_id = lax.axis_index("wide")
    rows = w_zx.shape[1]
    owned_gate_input = lax.dynamic_slice_in_dim(cotangent_gate_input, wide_id * rows, rows, 1)
    left_zx = (
        0.5 * left_statistic_gate
        + 0.5
        * jnp.einsum(
            "zko,zvo->zkv", owned_gate_input, cotangent_gate_input, precision=hyper_parameters
        )[:, None]
    )
    right_zx = 0.5 * stat_right_zx + 0.5 * jnp.einsum(
        "mdb,mdc->mbc", cotangent_gate_input, cotangent_gate_input, precision=hyper_parameters
    )
    update_step_gate = jnp.einsum(
        "nzf,nfu->nzu",
        inverse_root_left_gate[:, 0],
        cotangent_gate_input,
        precision=hyper_parameters,
    )
    update_step_gate = jnp.einsum(
        "yhp,ypu->yhu", update_step_gate, inverse_root_right_gate, precision=hyper_parameters
    )
    new_zx = w_zx - 0.5 * update_step_gate
    cols = w_out.shape[1]
    own_out = lax.dynamic_slice_in_dim(c_out, wide_id * cols, cols, 1)
    left_out = 0.5 * stat_left_out + 0.5 * jnp.dot(c_out, c_out.T, precision=hyper_parameters)
    right_out = (
        0.5 * stat_right_out + 0.5 * jnp.dot(own_out.T, c_out, precision=hyper_parameters)[None]
    )
    step_out = jnp.dot(
        jnp.dot(root_left_out, c_out, precision=hyper_parameters),
        root_right_out[0].T,
        precision=hyper_parameters,
    )
    new_out = w_out - 0.5 * step_out
    bc_rows = w_bc.shape[0]
    own_bc = lax.dynamic_slice_in_dim(c_bc, wide_id * bc_rows, bc_rows, 0)
    dt_rows = w_dt.shape[0]
    own_dt = lax.dynamic_slice_in_dim(c_dt, wide_id * dt_rows, dt_rows, 0)
    rate = 10.0
    return (
        block_out,
        in_grad,
        clip_norm,
        owned_gate_input,
        new_zx,
        left_zx,
        right_zx,
        own_out,
        new_out,
        left_out,
        right_out,
        own_bc,
        w_bc - rate * own_bc,
        own_dt,
        w_dt - rate * own_dt,
        c_cx,
        conv_x - rate * c_cx,
        c_cbc,
        conv_bc - rate * c_cbc,
        c_head,
        head_params - rate * c_head,
        c_og,
        out_gain - rate * c_og,
        c_ng,
        norm_gain - rate * c_ng,
    )


def solution(mesh):
    return jax.shard_map(
        local,
        mesh=mesh,
        in_specs=(
            P(("wide", "narrow"), None),
            P(("wide", "narrow"), None),
            P("wide"),
            P("narrow"),
            P(None, "wide", "narrow"),
            P("wide", None),
            P("wide", "narrow", None),
            P(None, "narrow"),
            P(),
            P(None, "narrow"),
            P("narrow"),
            P("narrow", "wide"),
            P(None, "narrow", "wide", None),
            P(None, "narrow", None),
            P("narrow", None),
            P("narrow", "wide", None),
            P(None, "narrow", "wide", None),
            P(None, "narrow", None),
            P("narrow", None),
            P("narrow", "wide", None),
        ),
        out_specs=(
            P(("wide", "narrow"), None),
            P(("wide", "narrow"), None),
            P(),
            P(None, "wide", "narrow"),
            P(None, "wide", "narrow"),
            P(None, "narrow", "wide", None),
            P(None, "narrow", None),
            P("narrow", "wide"),
            P("narrow", "wide"),
            P("narrow", None),
            P("narrow", "wide", None),
            P("wide", None),
            P("wide", None),
            P("wide", "narrow", None),
            P("wide", "narrow", None),
            P(None, "narrow"),
            P(None, "narrow"),
            P(),
            P(),
            P(None, "narrow"),
            P(None, "narrow"),
            P("narrow"),
            P("narrow"),
            P("narrow"),
            P("narrow"),
        ),
        check_vma=False,
    )
```

profile of v0, /device:TPU:0, one launch (start us, length us, event | category | flops | bytes accessed | tf_op | source)
XLA Modules:
  0.0 1050.5 jit_solution(8943865848705701343)
XLA Ops:
  15.6 8.4 all-reduce.39
  27.1 33.7 %all_gather.24 = f32[768,6,2]{1,2,0:T(2,128)S(1)} all-gather(f32[96,6,2]{1,2,0:T(2,128)S(1)} %copy.326), channel_id=1, replica_groups=mesh['wide'=8,'narrow'=4] {'wide'}, dimensions={0}, use_global_device_ids=true | all-gather | bytes 41472 | tf_op jit(solution)/shard_map/all_gather | solution.py:137
  61.3 36.0 %all_gather.23 = f32[768,256]{1,0:T(8,128)} all-gather(f32[96,256]{1,0:T(8,128)S(1)} %copy-done.84), channel_id=1, replica_groups=mesh['wide'=8,'narrow'=4] {'wide'}, dimensions={0}, use_global_device_ids=true | all-gather | bytes 884736 | tf_op jit(solution)/shard_map/all_gather | solution.py:136
  107.2 7.4 fusion.169
  147.5 6.4 rev.44
  160.1 20.2 %while.65 = (s32[]{:T(128)}, f32[1,6,64,64]{3,2,1,0:T(8,128)S(1)}, f32[8,1,6,64,64]{4,3,2,1,0:T(8,128)}, f32[8,1,6]{2,1,0:T(1,128)}, f32[8,1,6,64,64]{3,4,2,0,1:T(8,128)}, /*index=5*/s32[]{:T(128)}, s32[]{:T(128)}) while((s32[]{:T(128)}, f32[1,6,64,64]{3,2,1,0:T(8,128)S(1)}, f32[8,1,6,64,64]{4,3,2,1,0:T(8,128)}, ...), condition=%wide.region_6.7_spmd.clone, body=%wide.region_5.6_spmd.clone.sunk | while | flops 98307 | bytes 983220 | solution.py:48
  185.5 20.2 %while.64 = (s32[]{:T(128)}, f32[1,6,64,64]{3,2,1,0:T(8,128)S(1)}, f32[8,1,6,64,64]{4,3,2,1,0:T(8,128)}, f32[8,1,6]{2,1,0:T(1,128)}, f32[8,1,6,64,64]{3,4,2,0,1:T(8,128)}, /*index=5*/s32[]{:T(128)}, s32[]{:T(128)}) while((s32[]{:T(128)}, f32[1,6,64,64]{3,2,1,0:T(8,128)S(1)}, f32[8,1,6,64,64]{4,3,2,1,0:T(8,128)}, ...), condition=%wide.region_3.4_spmd.clone, body=%wide.region_2.3_spmd.clone.sunk | while | flops 98307 | bytes 983220 | solution.py:48
  216.2 6.6 fusion.52
  225.0 19.2 %reverse.1 = f32[1,1024,6,64]{1,0,3,2:T(1,128)} reverse(f32[1,1024,6,64]{1,0,3,2:T(1,128)} %bitcast.759), dimensions={1} | reverse | bytes 3145728
  250.4 6.6 fusion.49
  267.0 9.0 multiply_reduce_fusion.16
  281.7 8.3 fusion.102
  290.1 36.9 %reduce-scatter.2.cloned.1.call-done = f32[256,768]{1,0:T(8,128)} async-done(((f32[1024,768]{1,0:T(8,128)}), f32[256,768]{1,0:T(8,128)}) %reduce-scatter.2.cloned.1.call-update) | async-done | bytes 786448 | tf_op jit(solution)/shard_map/reduce_scatter | solution.py:168
  330.1 28.6 %all-gather.11.cloned.1.call-done = f32[1024,768]{1,0:T(8,128)} async-done(((f32[256,768]{1,0:T(8,128)}), f32[1024,768]{1,0:T(8,128)}) %all-gather.11.cloned.1.call-update) | async-done | bytes 3145744 | tf_op jit(solution)/shard_map/all_gather | solution.py:170
  358.7 8.9 multiply_reduce_fusion.10
  413.2 7.0 fusion.33
  422.2 53.5 %while.66 = (s32[]{:T(128)}, f32[1,6,64,64]{3,2,1,0:T(8,128)}, f32[8,1,6,64,64]{4,3,2,1,0:T(8,128)}, f32[8,1,6]{2,1,0:T(1,128)}, f32[8,1,6,64,64]{4,3,2,1,0:T(8,...) while((s32[]{:T(128)}, f32[1,6,64,64]{3,2,1,0:T(8,128)}, ...), condition=%wide.region_14.15_spmd.clone, body=%wide.region_12.14_spmd.clone.sunk | while | flops 122878 | bytes 1475343 | solution.py:48
  479.9 41.7 %while.67 = (s32[]{:T(128)}, f32[1,6,64,64]{3,2,1,0:T(8,128)S(1)}, f32[8,1,6,64,64]{4,3,2,1,0:T(8,128)}, f32[8,1,6]{2,1,0:T(1,128)}, f32[8,1,6,64,64]{4,3,2,1,0:...) while((s32[]{:T(128)}, f32[1,6,64,64]{3,2,1,0:T(8,128)S(1)}, ...), condition=%wide.region_18.19_spmd.clone, body=%wide.region_16.18_spmd.clone.sunk | while | flops 122878 | bytes 1475343 | solution.py:48
  534.9 12.0 %fusion.25 = (f32[8,6,128]{2,1,0:T(8,128)}, f32[8,6,128]{2,1,0:T(8,128)}, f32[8,6,128]{2,1,0:T(8,128)}, f32[8,128,128]{2,1,0:T(8,128)S(1)}, f32[8,128,128]{2,1,0...) fusion(f32[8,6,128]{2,1,0:T(8,128)S(1)} %copy-done.109, ...), kind=kOutput, calls=%fused_computation.60 | convolution fusion | flops 627273728 | bytes 8650752 | tf_op jit(solution)/shard_map/transpose(jvp(schtu,schup->schtp))/dot_general | solution.py:38
  564.7 19.2 %rev.50 = f32[1,1024,6,64]{1,0,3,2:T(1,128)} reverse(f32[1,1024,6,64]{1,0,3,2:T(1,128)} %bitcast.762), dimensions={1} | reverse | bytes 3145728 | tf_op jit(solution)/shard_map/transpose(jvp(jit(_flip)))/rev | solution.py:89
  596.4 7.4 reduce_window_sum.36
  606.9 7.4 reduce_window_sum.37
  620.8 6.8 fusion.174
  635.2 6.6 fusion.226
  652.5 7.0 fusion.5
  659.8 7.5 convolution_bitcast_fusion.4
  682.8 40.4 %psum.103 = f32[4,256]{1,0:T(4,128)S(1)} all-reduce(f32[4,256]{1,0:T(4,128)S(1)} %pad_add_fusion.9), channel_id=1, replica_groups=mesh['wide'=8,'narrow'=4] {'wide','narrow'}, use_global_device_ids=true, to_apply=%region_65.66 | all-reduce | flops 1024 | bytes 8192 | tf_op jit(solution)/shard_map/psum | solution.py:191
  728.5 43.5 %all-reduce.48.cloned.1.call-done = f32[768,256]{1,0:T(8,128)} async-done(((f32[768,256]{1,0:T(8,128)}), f32[768,256]{1,0:T(8,128)}) %all-reduce.48.cloned.1.call-update) | async-done | bytes 786448 | tf_op jit(solution)/shard_map/psum | solution.py:191
  775.3 66.6 %all-reduce.46.cloned.1.call-done = f32[1024,768]{1,0:T(8,128)} async-done(((f32[1024,768]{1,0:T(8,128)}), f32[1024,768]{1,0:T(8,128)}) %all-reduce.46.cloned.1.call-update) | async-done | bytes 3145744 | tf_op jit(solution)/shard_map/psum | solution.py:178
  845.7 40.3 %all-reduce.40 = (f32[768,6,2]{0,1,2:T(8,128)S(1)}, f32[4,384]{1,0:T(4,128)S(1)}, f32[5,6]{1,0:T(8,128)S(1)}, f32[384]{0:T(512)S(1)}, f32[192]{0:T(256)S(1)}) all-reduce(f32[768,6,2]{0,1,2:T(8,128)S(1)} %fusion.6, f32[4,384]{1,0:T(4,128)S(1)} %pad_add_fusion.8, ...), channel_id=1, replica_groups=mesh['wide'=8,'narrow'=4] {'wide'}, use_global_device_ids=true, to_apply=%region_38.39 | all-reduce | flops 11358 | bytes 90864 | tf_op jit(solution)/shard_map/psum | solution.py:188
  889.0 98.0 %all-reduce.50.cloned.1.call-done = (f32[2,768,384]{2,1,0:T(8,128)}, f32[384,768]{1,0:T(8,128)}) async-done(((f32[2,768,384]{2,1,0:T(8,128)}, f32[384,768]{1,0:T(8,128)}), (f32[2,768,384]{2,1,0:T(8,128)}, f32[384,768]{1,0:T(8,128)})) %all-reduce.50.cloned.1.call-update) | async-done | bytes 3538960 | tf_op jit(solution)/shard_map/psum | solution.py:188
  999.3 7.3 psum.101
  (755 shorter events, 430.8 us)
Async XLA Ops:
  7.2 1027.1 %copy-start = (f32[2,384,384]{2,1,0:T(8,128)S(1)}, f32[2,384,384]{2,1,0:T(8,128)}, u32[]{:S(2)}) copy-start(f32[2,384,384]{2,1,0:T(8,128)} %param.45) | copy-start | bytes 3538948
  7.2 54.0 %copy-start.84 = (f32[96,256]{1,0:T(8,128)S(1)}, f32[96,256]{1,0:T(8,128)}, u32[]{:S(2)}) copy-start(f32[96,256]{1,0:T(8,128)} %param.33) | copy-start | bytes 294916
  7.2 90.0 %all-gather.5.cloned.1.call-start = ((), (), s32[]{:S(2)}) async-start(), calls=%async_computation.1 | async-start | bytes 3932160 | tf_op jit(solution)/shard_map/all_gather | solution.py:141
  8.0 99.2 %all-gather.7.cloned.1.call-start = ((), (), s32[]{:S(2)}) async-start(), calls=%async_computation.2 | async-start | bytes 2654208 | tf_op jit(solution)/shard_map/all_gather | solution.py:135
  8.7 273.0 %all-gather.9.cloned.1.call-start = ((), (), s32[]{:S(2)}) async-start(), calls=%async_computation.3 | async-start | bytes 1327104 | tf_op jit(solution)/shard_map/all_gather | solution.py:138
  9.4 317.6 %reduce-scatter.2.cloned.1.call-start = ((), (), s32[]{:S(2)}) async-start(), calls=%async_computation.4 | async-start | bytes 3932160 | tf_op jit(solution)/shard_map/reduce_scatter | solution.py:168
  11.5 92.2 %copy-start.141 = (f32[6,2]{0,1:T(2,128)}, f32[6,2]{0,1:T(2,128)S(1)}, u32[]{:S(2)}) copy-start(f32[6,2]{0,1:T(2,128)S(1)} %get-tuple-element.807) | copy-start | bytes 148
  12.8 101.8 %copy-start.106 = (f32[1024]{0:T(1024)}, f32[1024]{0:T(1024)S(1)}, u32[]{:S(2)}) copy-start(f32[1024]{0:T(1024)S(1)} %fusion.216) | copy-start | bytes 12292
  25.4 109.5 %copy-start.143 = (f32[1,256]{1,0:T(1,128)}, f32[1,256]{1,0:T(1,128)S(1)}, u32[]{:S(2)}) copy-start(f32[1,256]{1,0:T(1,128)S(1)} %get-tuple-element.808) | copy-start | bytes 3076
  26.2 88.4 %copy-start.127 = (f32[384]{0:T(512)}, f32[384]{0:T(512)S(1)}, u32[]{:S(2)}) copy-start(f32[384]{0:T(512)S(1)} %get-tuple-element.691) | copy-start | bytes 4612
  26.3 88.4 %copy-start.129 = (f32[384]{0:T(512)}, f32[384]{0:T(512)S(1)}, u32[]{:S(2)}) copy-start(f32[384]{0:T(512)S(1)} %get-tuple-element.692) | copy-start | bytes 4612
  26.3 88.4 %copy-start.131 = (f32[384]{0:T(512)}, f32[384]{0:T(512)S(1)}, u32[]{:S(2)}) copy-start(f32[384]{0:T(512)S(1)} %get-tuple-element.693) | copy-start | bytes 4612
  26.3 88.4 %copy-start.133 = (f32[384]{0:T(512)}, f32[384]{0:T(512)S(1)}, u32[]{:S(2)}) copy-start(f32[384]{0:T(512)S(1)} %get-tuple-element.694) | copy-start | bytes 4612
  60.8 38.8 %copy-start.42 = (f32[768,6,2]{1,2,0:T(2,128)}, f32[768,6,2]{1,2,0:T(2,128)S(1)}, u32[]{:S(2)}) copy-start(f32[768,6,2]{1,2,0:T(2,128)S(1)} %all_gather.24) | copy-start | bytes 110596
  107.0 19.5 %copy-start.56 = (f32[1,8,6,128]{3,1,2,0:T(8,128)}, f32[1,8,6,128]{3,1,2,0:T(8,128)S(1)}, u32[]{:S(2)}) copy-start(f32[1,8,6,128]{3,1,2,0:T(8,128)S(1)} %reduce_window_sum.35) | copy-start | bytes 73732
  126.7 29.2 %copy-start.86 = (f32[8,6,128]{2,1,0:T(8,128)}, f32[8,6,128]{2,1,0:T(8,128)S(1)}, u32[]{:S(2)}) copy-start(f32[8,6,128]{2,1,0:T(8,128)S(1)} %copy.357) | copy-start | bytes 73732
  222.9 27.4 %copy-start.112 = (f32[8,6,128]{2,1,0:T(8,128)}, f32[8,6,128]{2,1,0:T(8,128)S(1)}, u32[]{:S(2)}) copy-start(f32[8,6,128]{2,1,0:T(8,128)S(1)} %copy.333) | copy-start | bytes 73732
  222.9 27.4 %copy-start.114 = (f32[8,6,128]{2,1,0:T(8,128)}, f32[8,6,128]{2,1,0:T(8,128)S(1)}, u32[]{:S(2)}) copy-start(f32[8,6,128]{2,1,0:T(8,128)S(1)} %copy.330) | copy-start | bytes 73732
  290.0 68.7 %all-gather.11.cloned.1.call-start = ((), (), s32[]{:S(2)}) async-start(), calls=%async_computation.5 | async-start | bytes 3932160 | tf_op jit(solution)/shard_map/all_gather | solution.py:170
  330.0 442.0 %all-reduce.48.cloned.1.call-start = ((), (), s32[]{:S(2)}) async-start(), calls=%async_computation.7 | async-start | bytes 1572864 | tf_op jit(solution)/shard_map/psum | solution.py:191
  564.7 19.2 %copy-start.13 = (f32[1024,384]{0,1:T(8,128)S(1)}, f32[1024,384]{0,1:T(8,128)}, u32[]{:S(2)}) copy-start(f32[1024,384]{0,1:T(8,128)} %copy.371) | copy-start | bytes 4718596
  641.8 200.1 %all-reduce.46.cloned.1.call-start = ((), (), s32[]{:S(2)}) async-start(), calls=%async_computation.6 | async-start | bytes 6291456 | tf_op jit(solution)/shard_map/psum | solution.py:178
  659.6 327.5 %all-reduce.50.cloned.1.call-start = ((), (), s32[]{:S(2)}) async-start(), calls=%async_computation.8 | async-start | bytes 7077888 | tf_op jit(solution)/shard_map/psum | solution.py:188
  681.6 41.6 %copy-start.155 = (f32[6,2]{0,1:T(2,128)S(1)}, f32[6,2]{0,1:T(2,128)}, u32[]{:S(2)}) copy-start(f32[6,2]{0,1:T(2,128)} %get-tuple-element.795) | copy-start | bytes 148
  681.6 42.3 %copy-start.156 = (f32[6,2]{0,1:T(2,128)S(1)}, f32[6,2]{0,1:T(2,128)}, u32[]{:S(2)}) copy-start(f32[6,2]{0,1:T(2,128)} %get-tuple-element.767) | copy-start | bytes 148
  775.2 70.3 %copy-start.103 = (f32[1024]{0:T(1024)S(1)}, f32[1024]{0:T(1024)}, u32[]{:S(2)}) copy-start(f32[1024]{0:T(1024)} %copy-done.102) | copy-start | bytes 12292
  775.2 70.4 %copy-start.154 = (f32[384]{0:T(512)S(1)}, f32[384]{0:T(512)}, u32[]{:S(2)}) copy-start(f32[384]{0:T(512)} %get-tuple-element.675) | copy-start | bytes 4612
  886.0 106.2 %copy-start.99 = (f32[768,6,2]{0,1,2:T(8,128)}, f32[768,6,2]{0,1,2:T(8,128)S(1)}, u32[]{:S(2)}) copy-start(f32[768,6,2]{0,1,2:T(8,128)S(1)} %get-tuple-element.743) | copy-start | bytes 110596
  886.0 106.2 %copy-start.125 = (f32[4,384]{1,0:T(4,128)}, f32[4,384]{1,0:T(4,128)S(1)}, u32[]{:S(2)}) copy-start(f32[4,384]{1,0:T(4,128)S(1)} %get-tuple-element.744) | copy-start | bytes 18436
  886.0 106.2 %copy-start.138 = (f32[5,6]{1,0:T(8,128)}, f32[5,6]{1,0:T(8,128)S(1)}, u32[]{:S(2)}) copy-start(f32[5,6]{1,0:T(8,128)S(1)} %get-tuple-element.745) | copy-start | bytes 364
  886.0 106.2 %copy-start.152 = (f32[384]{0:T(512)}, f32[384]{0:T(512)S(1)}, u32[]{:S(2)}) copy-start(f32[384]{0:T(512)S(1)} %get-tuple-element.746) | copy-start | bytes 4612
  886.0 106.2 %copy-start.163 = (f32[192]{0:T(256)}, f32[192]{0:T(256)S(1)}, u32[]{:S(2)}) copy-start(f32[192]{0:T(256)S(1)} %get-tuple-element.747) | copy-start | bytes 2308
  (141 other events, 669.1 us)
Sparse Core Ops, SparseCore 0:
  9.6 31.2 all-gather.4
  43.1 59.2 all-gather.6
  104.6 41.4 all-gather.8
  290.2 36.8 reduce-scatter.1
  330.1 28.5 all-gather.10
  641.9 130.0 all-reduce.47
  774.4 67.4 all-reduce.45
  846.1 140.9 all-reduce.49
where the time goes:
time: 1060 us; the launch traced here: 1050 us
  waiting for transfers between devices  276 us (26%)
  local copies, waits for them, and re-layouts  244 us (23%)
  matrix products  205 us (19%)
  blocking collectives  178 us (17%)
  other arithmetic  121 us (11%)
  between operations  25.6 us (2%)
    psum x1, waiting for transfers between devices, local(): lax.psum((d_zx, grad_out, d_dt, d_convx, d_head, grad_ogain, grad_ngain),...  98 us
    psum x1, waiting for transfers between devices, local(): dnormed = lax.psum(d_normed, 'narrow')  66.6 us
    unnamed x352, local copies, waits for them, and re-layouts  49.1 us
    psum x1, waiting for transfers between devices, local(): g_bc, g_cbc = lax.psum((d_bc, d_convbc), ('wide', 'narrow'))  43.5 us
    psum x1, blocking collectives, local(): g_bc, g_cbc = lax.psum((d_bc, d_convbc), ('wide', 'narrow'))  40.4 us
    psum x1, blocking collectives, local(): lax.psum((d_zx, grad_out, d_dt, d_convx, d_head, grad_ogain, grad_ngain),...  40.3 us
    dot_general x6, matrix products, scan_ssd(): jnp.einsum('schtu,schup->schtp', weights, xq, precision=hyper_parameters)  40.2 us
    reduce_scatter x1, waiting for transfers between devices, local(): lax.psum_scatter(partial_value, 'narrow', scatter_dimension=0, tiled=True)  36.9 us
  transfers between devices with their start and end apart: 8, of which 5 were waited for; matrix products, arithmetic and copies ran while one was open for 22% of the time, Pallas kernels for 0%

commit v1 on v0

v1 whole, which is shorter than its diff:
```python
import functools

import jax
import jax.numpy as jnp
from jax import lax
from jax.experimental import pallas as pl
from jax.experimental.pallas import tpu as pltpu
from jax.sharding import PartitionSpec as P

SPAN = 128
WIDTH = 64
HIGH = lax.Precision.HIGH
F32 = jnp.float32
NN = (((1,), (0,)), ((), ()))
NT = (((1,), (1,)), ((), ()))
TN = (((0,), (0,)), ((), ()))
TT = (((0,), (1,)), ((), ()))


def dot(a, b, dims=NN):
    return lax.dot_general(a, b, dims, precision=HIGH, preferred_element_type=F32)


def halves(v):
    hi = v.astype(jnp.bfloat16)
    return hi, (v - hi.astype(F32)).astype(jnp.bfloat16)


def product(a, b, dims=NN):
    (ah, al), (bh, bl) = a, b
    (left,), (right,) = dims[0]
    return lax.dot_general(
        jnp.concatenate([ah, al, ah], axis=left),
        jnp.concatenate([bh, bh, bl], axis=right),
        dims,
        preferred_element_type=F32,
    )


def dot3(a, b, dims=NN):
    return product(halves(a), halves(b), dims)


def sigmoid(v):
    return 1.0 / (1.0 + jnp.exp(-v))


def split3(v):
    hi = v.astype(jnp.bfloat16)
    rest = v - hi.astype(F32)
    mid = rest.astype(jnp.bfloat16)
    lo = (rest - mid.astype(F32)).astype(jnp.bfloat16)
    return jnp.concatenate([hi, mid, lo], axis=0)


def exact_dot(v, ones):
    rows = v.shape[0]
    out = lax.dot_general(split3(v), ones, NN, preferred_element_type=F32)
    return out[0:rows] + out[rows : 2 * rows] + out[2 * rows : 3 * rows]


def iota(shape, axis):
    return lax.broadcasted_iota(jnp.int32, shape, axis)


def shift_right(v, count):
    return jnp.where(iota(v.shape, 1) >= count, pltpu.roll(v, count, axis=1), 0.0)


def shift_left(v, count):
    length = v.shape[1]
    return jnp.where(iota(v.shape, 1) < length - count, pltpu.roll(v, length - count, axis=1), 0.0)


def conv_rows(v, taps):
    count = taps.shape[1]
    total = taps[:, count - 1 : count] * v
    for j in range(count - 1):
        total = total + taps[:, j : j + 1] * shift_right(v, count - 1 - j)
    return total


def pieces(ref, chans, state):
    bc = 2 * chans
    dt = bc + 4 * state
    return ref.at[0:chans], ref.at[chans:bc], ref.at[bc:dt], ref.at[dt : dt + 16]


def convolve(x_ref, bc_ref, live_ref, cx_ref, cbc_ref, xc_ref, dx_act_ref, b_ref, c_ref, dbc_act_ref):
    chans, tokens = xc_ref.shape
    state = c_ref.shape[0] // 2
    live = live_ref[...]

    def conv_x_rows(i, _):
        rows = pl.ds(pl.multiple_of(i * 8, 8), 8)
        u = conv_rows(x_ref[rows, :], cx_ref[rows, :])
        s = sigmoid(u)
        xc_ref[rows, :] = u * s * live
        dx_act_ref[rows, :] = (s + u * s * (1.0 - s)) * live
        return 0

    lax.fori_loop(0, chans // 8, conv_x_rows, 0, unroll=2)

    def conv_bc_rows(i, _, src, dst, dst_row, shift):
        rows = pl.ds(pl.multiple_of(src * state + i * 8, 8), 8)
        out = pl.ds(pl.multiple_of(dst_row + i * 8, 8), 8)
        u = conv_rows(bc_ref[rows, :], cbc_ref[rows, :])
        s = sigmoid(u)
        dbc_act_ref[rows, :] = s + u * s * (1.0 - s)
        v = u * s
        if shift == 1:
            v = shift_right(v, 1)
        if shift == -1:
            v = shift_left(v, 1)
        dst[out, :] = v
        return 0

    for src, dst, row, shift in ((0, b_ref, 0, 0), (1, c_ref, 0, 1), (2, b_ref, state, 0), (3, c_ref, state, -1)):
        lax.fori_loop(
            0,
            state // 8,
            functools.partial(conv_bc_rows, src=src, dst=dst, dst_row=row, shift=shift),
            0,
            unroll=2,
        )


def step_sizes(pre_ref, hp_ref, step_ref, cum_ref, cumex_ref, heads):
    blocks = pre_ref.shape[1] // SPAN
    pre = pre_ref[...] + hp_ref[:, 0:1]
    steps = jnp.maximum(pre, 0.0) + jnp.log1p(jnp.exp(-jnp.abs(pre)))
    step_ref[...] = steps
    logs = -hp_ref[:, 1:2] * steps
    rows16 = iota((16, SPAN), 0)
    lane16 = iota((16, SPAN), 1)
    row_q = iota((SPAN, SPAN), 0)
    lane_q = iota((SPAN, SPAN), 1)
    upto = (row_q <= lane_q).astype(F32).astype(jnp.bfloat16)
    downto = (row_q >= lane_q).astype(F32).astype(jnp.bfloat16)
    both = jnp.concatenate([upto, downto], axis=1)
    for b in range(blocks):
        sums = exact_dot(logs[:, b * SPAN : (b + 1) * SPAN], both)
        cum = jnp.where(rows16 < heads, sums[:, 0:SPAN], sums[:, SPAN : 2 * SPAN])
        ex_f = jnp.where(lane16 >= 1, pltpu.roll(cum, 1, axis=1), 0.0)
        ex_r = jnp.where(lane16 < SPAN - 1, pltpu.roll(cum, SPAN - 1, axis=1), 0.0)
        cum_ref[:, b * SPAN : (b + 1) * SPAN] = cum
        cumex_ref[:, b * SPAN : (b + 1) * SPAN] = jnp.where(rows16 < heads, ex_f, ex_r)


def states(xc_ref, b_ref, step_ref, cum_ref, sloc_ref, hcat_ref, heads):
    blocks = xc_ref.shape[1] // SPAN
    state = b_ref.shape[0] // 2

    def local_states(b, _):
        sl = pl.ds(pl.multiple_of(b * SPAN, SPAN), SPAN)
        bcat = spread(b_ref[:, sl], state)
        tail = tails(cum_ref[:, sl], step_ref[:, sl], heads)
        left = tailed(xc_ref[:, sl], tail, range(heads), heads)
        sloc_ref[b] = dot3(left, bcat, NT)
        return 0

    lax.fori_loop(0, blocks, local_states, 0)

    lane_h = iota((WIDTH, 2 * state), 1)
    for h in range(heads):
        rows = slice(h * WIDTH, (h + 1) * WIDTH)
        carry = jnp.zeros((WIDTH, 2 * state), F32)
        for i in range(blocks):
            r = blocks - 1 - i
            hcat_ref[i, rows, 0:state] = carry[:, 0:state]
            hcat_ref[r, rows, state : 2 * state] = carry[:, state : 2 * state]
            tot_f = jnp.exp(cum_ref[h : h + 1, (i + 1) * SPAN - 1 : (i + 1) * SPAN])
            tot_r = jnp.exp(cum_ref[heads + h : heads + h + 1, r * SPAN : r * SPAN + 1])
            factor = jnp.where(lane_h < state, tot_f, tot_r)
            piece = jnp.where(lane_h < state, sloc_ref[i, rows, :], sloc_ref[r, rows, :])
            carry = carry * factor + piece


def outputs(z_ref, xc_ref, b_ref, c_ref, step_ref, cum_ref, cumex_ref, hcat_ref, hp_ref, y_ref, inner_ref, heads, emit):
    blocks = xc_ref.shape[1] // SPAN
    state = b_ref.shape[0] // 2
    row_q = iota((SPAN, SPAN), 0)
    lane_q = iota((SPAN, SPAN), 1)
    lower = row_q < lane_q
    diag = row_q == lane_q

    def block(b, _):
        sl = pl.ds(pl.multiple_of(b * SPAN, SPAN), SPAN)
        bb, cc = b_ref[:, sl], c_ref[:, sl]
        inner = jnp.where(
            lower, dot3(bb[0:state], cc[0:state], TN), dot3(bb[state:], cc[state:], TN)
        )
        inner_ref[b] = inner
        cum, steps, cumex = cum_ref[:, sl], step_ref[:, sl], cumex_ref[:, sl]
        scale = jnp.exp(cumex)
        cols = columns(cum, steps)
        sums = None
        entering = dot3(hcat_ref[b], spread(cc, state))
        x_parts = halves(xc_ref[:, sl])
        for h in range(heads):
            rows = slice(h * WIDTH, (h + 1) * WIDTH)
            decay = decays(cols, cumex, lower, diag, h, heads)
            mt = jnp.where(diag, hp_ref[h : h + 1, 2:3], inner * decay)
            y = product((x_parts[0][rows], x_parts[1][rows]), halves(mt))
            y = y + entering[rows, 0:SPAN] * scale[h : h + 1]
            y = y + entering[rows, SPAN:] * scale[heads + h : heads + h + 1]
            z = z_ref[rows, sl]
            y_ref[rows, sl] = y
            sums = emit(b, sl, h, rows, y * (z * sigmoid(z)), sums)
        return 0

    lax.fori_loop(0, blocks, block, 0)


def fwd_kernel(
    heads,
    proj_ref,
    live_ref,
    cx_ref,
    cbc_ref,
    hp_ref,
    y_ref,
    xc_ref,
    dx_act_ref,
    b_ref,
    c_ref,
    dbc_act_ref,
    step_ref,
    cum_ref,
    cumex_ref,
    hcat_ref,
    inner_ref,
    gated_ref,
    sq_ref,
    sloc_ref,
):
    z_ref, x_ref, bc_ref, pre_ref = pieces(proj_ref, xc_ref.shape[0], c_ref.shape[0] // 2)
    convolve(x_ref, bc_ref, live_ref, cx_ref, cbc_ref, xc_ref, dx_act_ref, b_ref, c_ref, dbc_act_ref)
    step_sizes(pre_ref, hp_ref, step_ref, cum_ref, cumex_ref, heads)
    states(xc_ref, b_ref, step_ref, cum_ref, sloc_ref, hcat_ref, heads)

    def emit(b, sl, h, rows, gated, total):
        gated_ref[rows, sl] = gated
        part = jnp.sum(gated * gated, axis=0, keepdims=True)
        total = part if total is None else total + part
        if h == heads - 1:
            sq_ref[:, sl] = total
        return total

    outputs(z_ref, xc_ref, b_ref, c_ref, step_ref, cum_ref, cumex_ref, hcat_ref, hp_ref, y_ref, inner_ref, heads, emit)


def spread(bb, state):
    zero = jnp.zeros((state, SPAN), F32)
    top = jnp.concatenate([bb[0:state], zero], axis=1)
    low = jnp.concatenate([zero, bb[state:]], axis=1)
    return jnp.concatenate([top, low], axis=0)


def tails(cum, steps, heads):
    rows = iota((16, SPAN), 0)
    last = jnp.where(rows[:, 0:1] < heads, cum[:, SPAN - 1 : SPAN], cum[:, 0:1])
    return jnp.exp(last - cum) * steps


def tailed(xc, tail, chosen, heads):
    parts = []
    for i, h in enumerate(chosen):
        x = xc[i * WIDTH : (i + 1) * WIDTH]
        parts.append(
            jnp.concatenate([x * tail[h : h + 1], x * tail[heads + h : heads + h + 1]], axis=1)
        )
    return jnp.concatenate(parts, axis=0)


def columns(cum, steps):
    pad = jnp.zeros((SPAN - 32, SPAN), F32)
    return jnp.transpose(jnp.concatenate([cum, steps, pad], axis=0))


def decays(cols, cumex, lower, diag, h, heads):
    f, r = h, heads + h
    arg = jnp.where(
        lower, cumex[f : f + 1] - cols[:, f : f + 1], cumex[r : r + 1] - cols[:, r : r + 1]
    )
    step = jnp.where(lower, cols[:, 16 + f : 17 + f], cols[:, 16 + r : 17 + r])
    return jnp.where(diag, 0.0, jnp.exp(arg) * step)


def gate_back(z_ref, y_ref, don_ref, rms, coef, og_ref, dy_ref, dz_ref, dog_ref, onorm_ref=None):
    chans = y_ref.shape[0]

    def gate_rows(i, _):
        rows = pl.ds(pl.multiple_of(i * 8, 8), 8)
        z, y, don, og = z_ref[rows, :], y_ref[rows, :], don_ref[rows, :], og_ref[rows, :]
        s = sigmoid(z)
        act = z * s
        gated = y * act
        normed = rms * don
        dog_ref[rows, 0:1] = jnp.sum(gated * normed, axis=1, keepdims=True)
        dgated = normed * og - gated * coef
        dy_ref[rows, :] = dgated * act
        dz_ref[rows, :] = dgated * y * (s + act * (1.0 - s))
        if onorm_ref is not None:
            onorm_ref[rows, :] = gated * rms * og
        return 0

    lax.fori_loop(0, chans // 8, gate_rows, 0, unroll=2)


def back_intra(xc_ref, c_ref, inner_ref, step_ref, cum_ref, cumex_ref, hcat_ref, hp_ref, dy_s, dxc_s, dh_s, dc_s, din_s, g_s, cv_s, dd_s, chosen, heads, tick):
    blocks = xc_ref.shape[1] // SPAN
    state = c_ref.shape[0] // 2
    lower = iota((SPAN, SPAN), 0) < iota((SPAN, SPAN), 1)
    diag = iota((SPAN, SPAN), 0) == iota((SPAN, SPAN), 1)
    first = chosen[0] == 0

    def block(b, put):
        sl = pl.ds(pl.multiple_of(b * SPAN, SPAN), SPAN)
        cc = c_ref[:, sl]
        inner = inner_ref[b]
        cumex = cumex_ref[:, sl]
        scale = jnp.exp(cumex)
        cols = columns(cum_ref[:, sl], step_ref[:, sl])
        dinner = jnp.zeros((SPAN, SPAN), F32) if first else din_s[b]
        dcc = jnp.zeros((2 * state, SPAN), F32) if first else dc_s[:, sl]
        for h in chosen:
            f, r = h, heads + h
            rows = slice(h * WIDTH, (h + 1) * WIDTH)
            decay = decays(cols, cumex, lower, diag, h, heads)
            mt = inner * decay
            e_f, e_r = scale[f : f + 1], scale[r : r + 1]
            ce = jnp.concatenate([cc[0:state] * e_f, cc[state:] * e_r], axis=0)
            x = xc_ref[rows, sl]
            dy = dy_s[rows, sl]
            dy_parts = halves(dy)
            left = jnp.concatenate([x, hcat_ref[b, rows, :]], axis=1)
            back = product(halves(left), dy_parts, TN)
            dmt, dce = back[0:SPAN], back[SPAN:]
            dinner = dinner + dmt * decay
            w = dmt * mt
            over_f = jnp.sum(jnp.where(lower, w, 0.0), axis=0, keepdims=True)
            over_r = jnp.sum(jnp.where(lower, 0.0, w), axis=0, keepdims=True)
            prod = dce * ce
            put(g_s, (slice(f, f + 1), sl), over_f + jnp.sum(prod[0:state], axis=0, keepdims=True))
            put(g_s, (slice(r, r + 1), sl), over_r + jnp.sum(prod[state:], axis=0, keepdims=True))
            dcc = dcc + jnp.concatenate([dce[0:state] * e_f, dce[state:] * e_r], axis=0)
            right = jnp.concatenate(
                [jnp.where(lower, mt, 0.0), jnp.where(lower, 0.0, mt), ce], axis=0
            )
            out = product(dy_parts, halves(right), NT)
            dx_f, dx_r = out[:, 0:SPAN], out[:, SPAN : 2 * SPAN]
            put(dh_s, (b, rows, slice(None)), out[:, 2 * SPAN :])
            put(cv_s, (slice(f, f + 1), sl), jnp.sum(x * dx_f, axis=0, keepdims=True))
            put(cv_s, (slice(r, r + 1), sl), jnp.sum(x * dx_r, axis=0, keepdims=True))
            put(dd_s, (slice(h, h + 1), sl), jnp.sum(x * dy, axis=0, keepdims=True))
            put(dxc_s, (rows, sl), dx_f + dx_r + hp_ref[h : h + 1, 2:3] * dy)
        put(din_s, (b,), dinner)
        put(dc_s, (slice(None), sl), dcc)

    two_at_a_time(blocks, block, tick)


def two_at_a_time(blocks, block, tick):
    def body(i, _):
        stores = []
        for b in (2 * i, 2 * i + 1):
            block(b, lambda ref, at, value: stores.append((ref, at, value)))
        for ref, at, value in stores:
            ref[at] = value
        tick(2 * i)
        tick(2 * i + 1)
        return 0

    lax.fori_loop(0, blocks // 2, body, 0)


def back_states(cum_ref, hcat_ref, dh_s, tq_s, state, chosen, heads):
    blocks = hcat_ref.shape[0]
    lane_h = iota((WIDTH, 2 * state), 1)
    lane_1 = iota((1, 2 * state), 1)
    for h in chosen:
        rows = slice(h * WIDTH, (h + 1) * WIDTH)
        carry = jnp.zeros((WIDTH, 2 * state), F32)
        for i in range(blocks):
            f = blocks - 1 - i
            tot_f = jnp.exp(cum_ref[h : h + 1, (f + 1) * SPAN - 1 : (f + 1) * SPAN])
            tot_r = jnp.exp(cum_ref[heads + h : heads + h + 1, i * SPAN : i * SPAN + 1])
            factor = jnp.where(lane_h < state, tot_f, tot_r)
            direct = jnp.where(lane_h < state, dh_s[f, rows, :], dh_s[i, rows, :])
            kept = jnp.where(lane_h < state, hcat_ref[f, rows, :], hcat_ref[i, rows, :])
            scaled = carry * factor
            dots = jnp.sum(scaled * kept, axis=0, keepdims=True)
            q_f = jnp.sum(jnp.where(lane_1 < state, dots, 0.0), axis=1, keepdims=True)
            q_r = jnp.sum(jnp.where(lane_1 < state, 0.0, dots), axis=1, keepdims=True)
            tq_s[f, h : h + 1, :] = jnp.broadcast_to(q_f, (1, SPAN))
            tq_s[i, heads + h : heads + h + 1, :] = jnp.broadcast_to(q_r, (1, SPAN))
            dh_s[f, rows, 0:state] = carry[:, 0:state]
            dh_s[i, rows, state:] = carry[:, state:]
            carry = scaled + direct


def back_inter(xc_ref, b_ref, step_ref, cum_ref, dxc_s, dh_s, db_s, v_s, chosen, heads, tick):
    blocks = xc_ref.shape[1] // SPAN
    state = b_ref.shape[0] // 2
    first = chosen[0] == 0
    group = slice(chosen[0] * WIDTH, (chosen[-1] + 1) * WIDTH)

    def block(b, put):
        sl = pl.ds(pl.multiple_of(b * SPAN, SPAN), SPAN)
        bcat = spread(b_ref[:, sl], state)
        tail = tails(cum_ref[:, sl], step_ref[:, sl], heads)
        xc = xc_ref[group, sl]
        dxc = dxc_s[group, sl]
        dsl = halves(dh_s[b, group, :])
        dleft = product(dsl, halves(bcat))
        dbs = product(dsl, halves(tailed(xc, tail, chosen, heads)), TN)
        db = jnp.concatenate([dbs[0:state, 0:SPAN], dbs[state:, SPAN:]], axis=0)
        put(db_s, (slice(None), sl), db if first else db_s[:, sl] + db)
        parts = []
        for i, h in enumerate(chosen):
            f, r = h, heads + h
            part = slice(i * WIDTH, (i + 1) * WIDTH)
            tx_f = dleft[part, 0:SPAN] * tail[f : f + 1]
            tx_r = dleft[part, SPAN:] * tail[r : r + 1]
            put(v_s, (slice(f, f + 1), sl), jnp.sum(xc[part] * tx_f, axis=0, keepdims=True))
            put(v_s, (slice(r, r + 1), sl), jnp.sum(xc[part] * tx_r, axis=0, keepdims=True))
            parts.append(dxc[part] + tx_f + tx_r)
        put(dxc_s, (group, sl), jnp.concatenate(parts, axis=0))

    two_at_a_time(blocks, block, tick)


def back_logs(b_ref, c_ref, pre_ref, step_ref, hp_ref, ddt_ref, dhp_ref, db_s, dc_s, din_s, g_s, cv_s, v_s, dd_s, tq_s, heads):
    blocks = pre_ref.shape[1] // SPAN
    state = b_ref.shape[0] // 2
    row_q = iota((SPAN, SPAN), 0)
    lane_q = iota((SPAN, SPAN), 1)
    lower = row_q < lane_q
    strict = (row_q > lane_q).astype(F32)
    weak = (row_q >= lane_q).astype(F32)
    strict_t = (row_q < lane_q).astype(F32)
    weak_t = (row_q <= lane_q).astype(F32)
    tri = jnp.concatenate(
        [
            jnp.concatenate([strict, strict_t], axis=1),
            jnp.concatenate([weak, weak_t], axis=1),
            jnp.concatenate([strict_t, strict], axis=1),
        ],
        axis=0,
    ).astype(jnp.bfloat16)
    rows16 = iota((16, SPAN), 0)
    used = rows16 < 2 * heads
    rate = hp_ref[:, 1:2]

    def block(b, carry):
        bias_sum, log_sum, skip_sum = carry
        sl = pl.ds(pl.multiple_of(b * SPAN, SPAN), SPAN)
        dinner = din_s[b]
        both = jnp.concatenate(
            [jnp.where(lower, dinner, 0.0), jnp.where(lower, 0.0, dinner)], axis=0
        )
        dc_s[:, sl] = dc_s[:, sl] + dot3(spread(b_ref[:, sl], state), both)
        db = dot3(c_ref[:, sl], both, NT)
        db_s[0:state, sl] = db_s[0:state, sl] + db[0:state, 0:SPAN]
        db_s[state:, sl] = db_s[state:, sl] + db[state:, SPAN:]
        g = jnp.where(used, g_s[:, sl], 0.0)
        c = jnp.where(used, cv_s[:, sl], 0.0)
        v = jnp.where(used, v_s[:, sl], 0.0)
        steps = step_ref[:, sl]
        sums = exact_dot(jnp.concatenate([g, -c, v], axis=1), tri)
        dlog = jnp.where(rows16 < heads, sums[:, 0:SPAN], sums[:, SPAN:])
        dlog = dlog + jnp.where(used, tq_s[b], 0.0)
        pre = pre_ref[:, sl] + hp_ref[:, 0:1]
        small = steps < 1e-30
        ratio = jnp.where(small, 1.0, sigmoid(pre) / jnp.where(small, 1.0, steps))
        dpre = (c + v) * ratio - rate * dlog * sigmoid(pre)
        ddt_ref[:, sl] = dpre
        skip = jnp.where(rows16 < heads, dd_s[:, sl], 0.0)
        return bias_sum + dpre, log_sum - rate * dlog * steps, skip_sum + skip

    zeros16 = jnp.zeros((16, SPAN), F32)
    bias_sum, log_sum, skip = lax.fori_loop(0, blocks, block, (zeros16, zeros16, zeros16))
    dhp_ref[:, 0:1] = jnp.sum(bias_sum, axis=1, keepdims=True)
    dhp_ref[:, 1:2] = jnp.sum(log_sum, axis=1, keepdims=True)
    dhp_ref[:, 2:3] = jnp.sum(skip, axis=1, keepdims=True)


def conv_back(du, v, taps):
    count = taps.shape[1]
    dv = taps[:, count - 1 : count] * du
    sums = [jnp.sum(du * v, axis=1, keepdims=True)]
    for j in range(count - 2, -1, -1):
        moved = shift_left(du, count - 1 - j)
        dv = dv + taps[:, j : j + 1] * moved
        sums.append(jnp.sum(moved * v, axis=1, keepdims=True))
    return dv, sums[::-1]


def conv_x_back(xin_ref, cx_ref, dx_act_ref, dxc_s, dxin_ref, dcx_ref, start, count):
    def group(i, _):
        rows = pl.ds(pl.multiple_of(start + i * 8, 8), 8)
        dv, sums = conv_back(dxc_s[rows, :] * dx_act_ref[rows, :], xin_ref[rows, :], cx_ref[rows, :])
        dxin_ref[rows, :] = dv
        for j, item in enumerate(sums):
            dcx_ref[rows, j : j + 1] = item
        return 0

    lax.fori_loop(0, count // 8, group, 0, unroll=2)


def conv_bc_back(bc_ref, cbc_ref, dbc_act_ref, db_s, dc_s, dbc_ref, dcbc_ref):
    state = db_s.shape[0] // 2

    def group(i, _, src, grad, grad_row, shift):
        rows = pl.ds(pl.multiple_of(src * state + i * 8, 8), 8)
        from_rows = pl.ds(pl.multiple_of(grad_row + i * 8, 8), 8)
        d = grad[from_rows, :]
        if shift == 1:
            d = shift_left(d, 1)
        if shift == -1:
            d = shift_right(d, 1)
        dv, sums = conv_back(d * dbc_act_ref[rows, :], bc_ref[rows, :], cbc_ref[rows, :])
        dbc_ref[rows, :] = dv
        for j, item in enumerate(sums):
            dcbc_ref[rows, j : j + 1] = item
        return 0

    for src, grad, row, shift in ((0, db_s, 0, 0), (1, dc_s, 0, 1), (2, db_s, state, 0), (3, dc_s, state, -1)):
        lax.fori_loop(
            0,
            state // 8,
            functools.partial(group, src=src, grad=grad, grad_row=row, shift=shift),
            0,
            unroll=2,
        )


def pairs_of(heads):
    return [tuple(range(h, min(h + 2, heads))) for h in range(0, heads, 2)]


def bwd_kernel(
    heads,
    proj_ref,
    y_ref,
    xc_ref,
    dx_act_ref,
    b_ref,
    c_ref,
    dbc_act_ref,
    step_ref,
    cum_ref,
    cumex_ref,
    hcat_ref,
    inner_ref,
    don_ref,
    rms_ref,
    coef_ref,
    og_ref,
    cx_ref,
    cbc_ref,
    hp_ref,
    dproj_ref,
    dcx_ref,
    dcbc_ref,
    dhp_ref,
    dog_ref,
    dy_s,
    dxc_s,
    dh_s,
    db_s,
    dc_s,
    din_s,
    g_s,
    cv_s,
    v_s,
    dd_s,
    tq_s,
):
    chans, state = y_ref.shape[0], b_ref.shape[0] // 2
    z_ref, xin_ref, bc_ref, pre_ref = pieces(proj_ref, chans, state)
    dz_ref, dxin_ref, dbc_ref, ddt_ref = pieces(dproj_ref, chans, state)
    gate_back(z_ref, y_ref, don_ref, rms_ref[...], coef_ref[...], og_ref, dy_s, dz_ref, dog_ref)
    for chosen in pairs_of(heads):
        back_intra(
            xc_ref, c_ref, inner_ref, step_ref, cum_ref, cumex_ref, hcat_ref, hp_ref, dy_s, dxc_s, dh_s, dc_s,
            din_s, g_s, cv_s, dd_s, chosen, heads, lambda b: None,
        )
        back_states(cum_ref, hcat_ref, dh_s, tq_s, state, chosen, heads)
        back_inter(xc_ref, b_ref, step_ref, cum_ref, dxc_s, dh_s, db_s, v_s, chosen, heads, lambda b: None)
    conv_x_back(xin_ref, cx_ref, dx_act_ref, dxc_s, dxin_ref, dcx_ref, 0, chans)
    back_logs(
        b_ref, c_ref, pre_ref, step_ref, hp_ref, ddt_ref, dhp_ref, db_s, dc_s, din_s, g_s, cv_s, v_s, dd_s, tq_s, heads
    )
    conv_bc_back(bc_ref, cbc_ref, dbc_act_ref, db_s, dc_s, dbc_ref, dcbc_ref)


def call(kernel, out_shapes, scratch, flops):
    return pl.pallas_call(
        kernel,
        out_shape=[jax.ShapeDtypeStruct(shape, F32) for shape in out_shapes],
        scratch_shapes=[pltpu.VMEM(shape, F32) for shape in scratch],
        compiler_params=pltpu.CompilerParams(vmem_limit_bytes=56 * 1024 * 1024),
        cost_estimate=pl.CostEstimate(flops=flops, bytes_accessed=20_000_000, transcendentals=0),
    )


def run_fwd(proj, live, cx, cbc, hp, heads):
    tokens = proj.shape[1]
    chans, n4 = cx.shape[0], cbc.shape[0]
    blocks = tokens // SPAN
    full, half, rows = (chans, tokens), (n4 // 2, tokens), (16, tokens)
    return call(
        functools.partial(fwd_kernel, heads),
        [full, full, full, half, half, (n4, tokens), rows, rows, rows, (blocks, chans, n4 // 2), (blocks, SPAN, SPAN), full, (1, tokens)],
        [(blocks, chans, n4 // 2)],
        2_000_000_000,
    )(proj, live, cx, cbc, hp)


def run_bwd(proj, kept, don, rms, coef, og, cx, cbc, hp, heads):
    tokens = proj.shape[1]
    chans, n4 = cx.shape[0], cbc.shape[0]
    blocks = tokens // SPAN
    full, half, rows = (chans, tokens), (n4 // 2, tokens), (16, tokens)
    return call(
        functools.partial(bwd_kernel, heads),
        [proj.shape, (chans, 4), (n4, 4), (16, 3), (chans, 1)],
        [full, full, (blocks, chans, n4 // 2), half, half, (blocks, SPAN, SPAN), rows, rows, rows, rows, (blocks, 16, SPAN)],
        4_000_000_000,
    )(proj, *kept, don, rms, coef, og, cx, cbc, hp)


def square_sum(arrays):
    total = jnp.float32(0.0)
    for item in arrays:
        total = total + jnp.sum(item * item)
    return total


def pad_rows(v):
    return jnp.concatenate([v, jnp.zeros((16 - v.shape[0],) + v.shape[1:], v.dtype)], axis=0)


def local(
    hidden_in,
    out_cot,
    lengths,
    norm_gain,
    w_zx,
    w_bc,
    w_dt,
    conv_x,
    conv_bc,
    head_params,
    out_gain,
    w_out,
    left_statistic_gate,
    stat_right_zx,
    stat_left_out,
    stat_right_out,
    inverse_root_left_gate,
    inverse_root_right_gate,
    root_left_out,
    root_right_out,
):
    rows, chans = w_zx.shape[1], w_zx.shape[2]
    heads = w_dt.shape[1]
    n4 = w_bc.shape[1]
    own_rows, width = hidden_in.shape
    narrow_id, wide_id = lax.axis_index("narrow"), lax.axis_index("wide")

    full_in = lax.all_gather(hidden_in, "narrow", axis=0, tiled=True)
    full_gain = lax.all_gather(norm_gain, "narrow", axis=0, tiled=True)
    dt_cols = jnp.transpose(w_dt, (0, 2, 1)).reshape(rows, 2 * heads)
    own_w = jnp.concatenate(
        [w_zx[0], w_zx[1], w_bc, dt_cols, jnp.zeros((rows, 16 - 2 * heads), F32)], axis=1
    )
    w_in = lax.all_gather(own_w, "wide", axis=0, tiled=True)
    wide_out = lax.all_gather(w_out, "wide", axis=1, tiled=True)

    tokens = full_in.shape[0]
    live = (jnp.arange(tokens) < lengths[0]).astype(F32)
    row_start = narrow_id * own_rows
    live_own = lax.dynamic_slice_in_dim(live, row_start, own_rows, 0)
    dbranch = lax.all_gather(live_own[:, None] * out_cot, "narrow", axis=0, tiled=True)

    inv_rms = lax.rsqrt(jnp.mean(full_in * full_in, axis=-1) + 1e-05)
    normed = full_in * inv_rms[:, None] * full_gain
    proj = dot(w_in, normed, TT)
    cx, cbc = conv_x.T, conv_bc.T
    hp = jnp.concatenate(
        [
            pad_rows(head_params[0:2].reshape(2 * heads, 1)),
            pad_rows(jnp.exp(head_params[2:4]).reshape(2 * heads, 1)),
            pad_rows(head_params[4].reshape(heads, 1)),
        ],
        axis=1,
    )
    *kept, gated, squares = run_fwd(proj, live[None, :], cx, cbc, hp, heads)
    donorm = dot(wide_out, dbranch, NT)
    inner = jnp.sum(gated * (donorm * out_gain[:, None]), axis=0, keepdims=True)
    stats = lax.psum(jnp.concatenate([squares, inner], axis=0), "narrow")
    inner_total = chans * lax.axis_size("narrow")
    rms = lax.rsqrt(stats[0:1] / inner_total + 1e-05)
    coef = rms**3 * stats[1:2] / inner_total
    onorm = gated * rms * out_gain[:, None]
    branch = lax.psum_scatter(dot(onorm, wide_out, TN), "narrow", scatter_dimension=0, tiled=True)
    block_out = hidden_in + live_own[:, None] * branch
    g_out = lax.psum(dot(onorm, dbranch), "wide")

    dproj, d_cx, d_cbc, d_hp, d_og = run_bwd(
        proj, kept, donorm, rms, coef, out_gain[:, None], cx, cbc, hp, heads
    )
    d_normed = dot(dproj, w_in, TT)
    d_w = dot(normed, dproj, TT)
    dnormed = lax.psum_scatter(d_normed, "narrow", scatter_dimension=0, tiled=True)
    own_inv = lax.dynamic_slice_in_dim(inv_rms, row_start, own_rows, 0)[:, None]
    total_dot = jnp.sum(hidden_in * full_gain * dnormed, axis=1, keepdims=True)
    in_grad = out_cot + (
        own_inv * full_gain * dnormed - hidden_in * (own_inv**3 * total_dot / width)
    )
    d_gain = jnp.sum(hidden_in * own_inv * dnormed, axis=0)

    g_zx = lax.psum(d_w[:, 0 : 2 * chans], "wide")
    g_dt, g_cx, g_hp, g_og = lax.psum((d_w[:, 2 * chans + n4 :], d_cx, d_hp, d_og), "wide")
    g_bc, g_cbc, g_gain = lax.psum(
        (d_w[:, 2 * chans : 2 * chans + n4], d_cbc, d_gain), ("wide", "narrow")
    )
    shard = norm_gain.shape[0]
    g_ng = lax.dynamic_slice_in_dim(g_gain, narrow_id * shard, shard, 0)
    g_dt = jnp.transpose(g_dt[:, 0 : 2 * heads].reshape(width, 2, heads), (0, 2, 1))
    g_cx, g_cbc, g_og = g_cx.T, g_cbc.T, g_og[:, 0]
    g_head = jnp.concatenate(
        [
            g_hp[0 : 2 * heads, 0].reshape(2, heads),
            g_hp[0 : 2 * heads, 1].reshape(2, heads),
            g_hp[0:heads, 2].reshape(1, heads),
        ],
        axis=0,
    )
    local_squares = square_sum((g_zx, g_out, g_dt, g_cx, g_head, g_og, g_ng))
    total_squares = lax.psum(local_squares, "narrow") + square_sum((g_bc, g_cbc))
    clip_norm = jnp.sqrt(total_squares)
    factor = 1.0 / jnp.maximum(clip_norm, 1.0)
    c_zx, c_out, c_bc, c_dt = g_zx * factor, g_out * factor, g_bc * factor, g_dt * factor
    c_cx, c_cbc, c_head, c_og, c_ng = (
        g_cx * factor,
        g_cbc * factor,
        g_head * factor,
        g_og * factor,
        g_ng * factor,
    )
    halves = (c_zx[:, 0:chans], c_zx[:, chans:])
    own_zx = lax.dynamic_slice_in_dim(c_zx, wide_id * rows, rows, 0)
    own_halves = (own_zx[:, 0:chans], own_zx[:, chans:])
    left_zx = jnp.stack(
        [
            0.5 * left_statistic_gate[m, 0] + 0.5 * dot(own_halves[m], halves[m], NT)
            for m in range(2)
        ]
    )[:, None]
    right_zx = jnp.stack(
        [0.5 * stat_right_zx[m] + 0.5 * dot(halves[m], halves[m], TN) for m in range(2)]
    )
    new_zx = jnp.stack(
        [
            w_zx[m]
            - 0.5
            * dot(dot(inverse_root_left_gate[m, 0], halves[m]), inverse_root_right_gate[m])
            for m in range(2)
        ]
    )
    cols = w_out.shape[1]
    own_out = lax.dynamic_slice_in_dim(c_out, wide_id * cols, cols, 1)
    left_out = 0.5 * stat_left_out + 0.5 * dot(c_out, c_out, NT)
    right_out = 0.5 * stat_right_out + 0.5 * dot(own_out, c_out, TN)[None]
    new_out = w_out - 0.5 * dot(dot(root_left_out, c_out), root_right_out[0], NT)
    own_bc = lax.dynamic_slice_in_dim(c_bc, wide_id * rows, rows, 0)
    own_dt = lax.dynamic_slice_in_dim(c_dt, wide_id * rows, rows, 0)
    rate = 10.0
    return (
        block_out,
        in_grad,
        clip_norm,
        jnp.stack(own_halves),
        new_zx,
        left_zx,
        right_zx,
        own_out,
        new_out,
        left_out,
        right_out,
        own_bc,
        w_bc - rate * own_bc,
        own_dt,
        w_dt - rate * own_dt,
        c_cx,
        conv_x - rate * c_cx,
        c_cbc,
        conv_bc - rate * c_cbc,
        c_head,
        head_params - rate * c_head,
        c_og,
        out_gain - rate * c_og,
        c_ng,
        norm_gain - rate * c_ng,
    )


MESH = pl.DeviceIdType.MESH
MIB = 1024 * 1024


class Place:
    def __init__(self, wide):
        self.wide = wide
        self.depth = wide // 2
        self.w, self.n = lax.axis_index("wide"), lax.axis_index("narrow")
        self.z, self.x = self.w // 2, self.w % 2
        self.y, self.c = self.n // 2, self.n % 2
        self.core = (self.w, self.y * 2 + 1 - self.c)
        self.row = (self.w, (1 - self.y) * 2 + self.c)
        self.corner = (self.w, (1 - self.y) * 2 + 1 - self.c)
        self.across = (self.z * 2 + 1 - self.x, self.n)

    def group(self):
        return [self.core, self.row, self.corner]

    def along(self, k):
        return ((self.z + k) % self.depth) * 2 + self.x, self.n

    def others(self, k):
        return (self.w + k) % self.wide, self.n


class Links:
    def __init__(self, send, recv):
        self.send, self.recv, self.count, self.started = send, recv, 0, []

    def plan(self, src, dst, device):
        i = self.count
        self.count = i + 1
        item = pltpu.make_async_remote_copy(
            src_ref=src,
            dst_ref=dst,
            send_sem=self.send.at[i],
            recv_sem=self.recv.at[i],
            device_id=device,
            device_id_type=MESH,
        )
        self.started.append(item)
        return item

    def copy(self, src, dst, device):
        item = self.plan(src, dst, device)
        item.start()
        return item

    def release(self, items):
        for item in items:
            item.wait_send()
        self.started = [item for item in self.started if all(item is not done for done in items)]

    def drain(self):
        self.release(list(self.started))


def arrived(copies):
    for item in copies:
        item.wait_recv()


def begin(copies):
    for item in copies:
        item.start()


def greet(devices):
    barrier = pltpu.get_barrier_semaphore()
    for device in devices:
        pl.semaphore_signal(barrier, inc=1, device_id=device, device_id_type=MESH)
    return lambda: pl.semaphore_wait(barrier, len(devices))


def as_row(col):
    return jnp.transpose(jnp.broadcast_to(col, (col.shape[0], 128)))[0:1]


def as_col(row):
    return jnp.transpose(jnp.broadcast_to(row, (128, 128)))[:, 0:1]


def flat(v):
    return v.reshape(-1, v.shape[-1])


class Piece:
    def __init__(self, here, links, part, x_rx, z_rx, full, square):
        self.here, self.part, self.x_rx, self.z_rx = here, part, x_rx, z_rx
        self.full, self.square = full, square
        steps = range(1, here.depth)
        place, column = full.at[here.z, here.x], full.at[:, here.x]
        self.first = links.plan(part.at[:, 1 - here.x], x_rx, here.across)
        self.second = [
            links.plan(x_rx.at[(here.z + k) % here.depth], z_rx.at[k - 1], here.along(k)) for k in steps
        ]
        self.third = [links.plan(place, place, here.along(k)) for k in steps]
        self.fourth = links.plan(column, column, here.across)

    def start(self):
        self.first.start()

    def fold(self):
        self.first.wait_recv()
        for k in range(self.here.depth):
            self.x_rx[k] = self.x_rx[k] + self.part[k, self.here.x]
        begin(self.second)

    def own(self):
        arrived(self.second)
        total = self.x_rx[self.here.z]
        for k in range(1, self.here.depth):
            total = total + self.z_rx[k - 1]
        self.full[self.here.z, self.here.x] = total
        begin(self.third)
        self.square[...] = jnp.broadcast_to(total_square(total), self.square.shape)

    def spread(self):
        arrived(self.third)
        self.fourth.start()

    def finish(self):
        self.fourth.wait_recv()


def total_square(v):
    return jnp.sum(jnp.sum(v * v, axis=0, keepdims=True), axis=1, keepdims=True)


def layer_kernel(
    wide,
    heads,
    shard,
    inner_total,
    length_ref,
    hidden_ref,
    cot_ref,
    gain_ref,
    w_ref,
    wout_ref,
    bcw_ref,
    dtw_ref,
    cx_in,
    cbc_in,
    hp_in,
    og_in,
    block_ref,
    grad_ref,
    gfull,
    bc_own,
    dt_own,
    sv_sum,
    norm_ref,
    hq,
    cq,
    wz_g,
    wx_g,
    wo_g,
    bc_g,
    dt_g,
    gain_g,
    dtt,
    gain_col,
    gain_row,
    turn_s,
    cx_ref,
    cbc_ref,
    hp_ref,
    og_ref,
    live_ref,
    inv_ref,
    proj,
    y_s,
    xc,
    dx_act,
    b_s,
    c_s,
    dbc_act,
    step_s,
    cum_s,
    cumex_s,
    hcat,
    inner_s,
    don,
    onorm,
    dy_s,
    dh_s,
    db_s,
    dc_s,
    din_s,
    g_s,
    cv_s,
    v_s,
    dd_s,
    tq_s,
    cols_s,
    dcbc_s,
    dhp_s,
    dog_s,
    dgain_s,
    stat_own,
    stat_g,
    part,
    x_rx,
    z_rx,
    core_rx,
    row_rx,
    gbc,
    bc_core,
    bc_row,
    bc_mine,
    bc_rx,
    gdt,
    dt_rx,
    shared_g,
    sv_g,
    norm_n,
    norm_w,
    square_s,
    hq_hi,
    hq_lo,
    wt_hi,
    wt_lo,
    send,
    recv,
    stat_send,
    stat_recv,
):
    here = Place(wide)
    links = Links(send, recv)
    w, n, z, x, y, c, depth = here.w, here.n, here.z, here.x, here.y, here.c, here.depth
    group = here.group()
    far = [here.others(k) for k in range(1, wide)]
    own_rows, width = hidden_ref.shape
    chans, tokens = y_s.shape
    state = b_s.shape[0] // 2
    blocks = tokens // SPAN
    parts = tokens // own_rows
    thirds = chans // 128
    z_ref, x_ref, bc_ref, pre_ref = pieces(proj, chans, state)
    met = greet(group + far)
    jobs = [
        Piece(
            here, links, part.at[i if i < 2 * thirds else i - thirds], x_rx.at[i], z_rx.at[i],
            gfull.at[i], square_s.at[i],
        )
        for i in range(3 * thirds)
    ]
    z_jobs, x_jobs, o_jobs = jobs[0:thirds], jobs[thirds : 2 * thirds], jobs[2 * thirds :]

    half = bcw_ref.shape[0] // 2
    wx_g[z, x] = w_ref[1]
    bc_g[z, x, c] = bcw_ref[pl.ds(pl.multiple_of(c * half, 8), half), :]
    dt_g[z, x] = jnp.zeros(dt_g.shape[2:], F32)
    for h in range(heads):
        for i in range(2):
            row = i * heads + h
            dt_g[z, x, row : row + 1, 0 : dtw_ref.shape[2]] = dtw_ref[h, i : i + 1, :]
    line = gain_ref[...].reshape(1, shard)
    gain_g[n] = jnp.zeros(gain_g.shape[1:], F32)
    for i in range((shard + 127) // 128):
        size = min(128, shard - 128 * i)
        gain_g[n, i : i + 1, 0:size] = line[:, 128 * i : 128 * i + size]
    squares = jnp.zeros((1, own_rows), F32)
    for i in range(width // 128):
        turned = jnp.transpose(hidden_ref[:, i * 128 : (i + 1) * 128])
        squares = squares + jnp.sum(turned * turned, axis=0, keepdims=True)
        hq[n, i * 128 : (i + 1) * 128, :] = turned
    inv_ref[...] = lax.rsqrt(squares / width + 1e-05)
    for i in range(width // 128):
        hq[n, i * 128 : (i + 1) * 128, :] = hq[n, i * 128 : (i + 1) * 128, :] * inv_ref[...]
    met()

    def along(ref):
        return [links.copy(ref, ref, here.along(k)) for k in range(1, depth)]

    def exchange(ref):
        return [links.copy(ref, ref, here.row), links.copy(ref, ref, here.core)]

    class Relay:
        def __init__(self, *views):
            self.views = views
            self.direct = [along(view(z)) for view in views]
            self.passed = []

        def begin(self):
            self.passed = [links.copy(view(z), view(z), here.across) for view in self.views]

        def forward(self):
            for k in range(1, depth):
                source = (z + depth - k) % depth
                for view, copies in zip(self.views, self.direct):
                    copies[k - 1].wait_recv()
                    self.passed.append(links.copy(view(source), view(source), here.across))

        def wait(self):
            arrived(self.passed)

    h_copies = exchange(hq.at[n])
    gain_copies = [links.copy(gain_g.at[n], gain_g.at[n], device) for device in group]
    first = Relay(
        lambda i: wx_g.at[i, x], lambda i: bc_g.at[i, x, c], lambda i: dt_g.at[i, x]
    )
    first.begin()

    wz_g[z, x] = w_ref[0]
    wo_g[z, x] = wout_ref[...]
    live_ref[...] = jnp.where(iota((1, tokens), 1) < length_ref[0], 1.0, 0.0)
    live_own = live_ref[:, pl.ds(pl.multiple_of(n * own_rows, 128), own_rows)]
    for i in range(width // 128):
        cq[n, i * 128 : (i + 1) * 128, :] = jnp.transpose(cot_ref[:, i * 128 : (i + 1) * 128]) * live_own
    turn_s[...] = jnp.zeros_like(turn_s)
    for ref, out in ((cx_in, cx_ref), (cbc_in, cbc_ref)):
        for i in range(ref.shape[1] // 128):
            turn_s[0:4, :] = ref[:, i * 128 : (i + 1) * 128]
            out[i * 128 : (i + 1) * 128, :] = jnp.transpose(turn_s[...])[:, 0:4]
    turn_s[...] = jnp.zeros_like(turn_s)
    turn_s[0:1, 0:heads] = hp_in[0:1, :]
    turn_s[0:1, heads : 2 * heads] = hp_in[1:2, :]
    turn_s[1:2, 0:heads] = jnp.exp(hp_in[2:3, :])
    turn_s[1:2, heads : 2 * heads] = jnp.exp(hp_in[3:4, :])
    turn_s[2:3, 0:heads] = hp_in[4:5, :]
    hp_ref[...] = jnp.transpose(turn_s[...])[0:16, 0:3]
    og_line = og_in[...].reshape(1, chans)
    for i in range(thirds):
        og_ref[i * 128 : (i + 1) * 128, :] = as_col(og_line[:, i * 128 : (i + 1) * 128])
    cols_s[...] = jnp.zeros_like(cols_s)
    dcbc_s[...] = jnp.zeros_like(dcbc_s)
    dhp_s[...] = jnp.zeros_like(dhp_s)

    def cut(q):
        hq_hi[q], hq_lo[q] = halves(hq[q])

    cut(n)
    h_copies[1].wait_recv()
    cut(here.core[1])
    first.forward()
    second = Relay(lambda i: wz_g.at[i, x])
    h_copies[0].wait_recv()
    other = here.row[1]
    h_far = links.copy(hq.at[other], hq.at[other], here.core)
    c_copies = exchange(cq.at[n])
    arrived(gain_copies)
    for q in range(parts):
        turned = jnp.transpose(jnp.concatenate([gain_g[q], jnp.zeros((120, 128), F32)], axis=0))
        for i in range((shard + 127) // 128):
            size = min(128, shard - 128 * i)
            start = shard * q + 128 * i
            gain_col[start : start + size, :] = turned[0:size, i : i + 1]
    for i in range(width // 128):
        gain_row[:, i * 128 : (i + 1) * 128] = as_row(gain_col[i * 128 : (i + 1) * 128, :])

    def turn(ref, row, scale=True):
        for i in range(ref.shape[-1] // 128):
            cols = flat(ref[..., i * 128 : (i + 1) * 128])
            if scale:
                cols = cols * gain_col[...]
            for dst, value in zip((wt_hi, wt_lo), halves(jnp.transpose(cols))):
                dst[row + i * 128 : row + (i + 1) * 128, :] = value

    def quarter(q):
        return pl.ds(pl.multiple_of(q * own_rows, 128), own_rows)

    def each_quarter(body):
        def step(q, _):
            body(q)
            return 0

        lax.fori_loop(0, parts, step, 0)

    def rows_of(start, stop):
        return wt_hi[start:stop, :], wt_lo[start:stop, :]

    def project(out_ref, weights):
        def body(q):
            out_ref[:, quarter(q)] = product(weights(), (hq_hi[q], hq_lo[q]))

        each_quarter(body)

    first.wait()
    second.begin()
    bc_core_copy = links.copy(bc_g.at[:, :, c], bc_g.at[:, :, c], here.core)
    turn(wx_g, chans)
    lanes = width // wide
    for i in range(wide):
        dtt[:, i * lanes : (i + 1) * lanes] = dt_g[i // 2, i % 2][:, 0:lanes]
    h_far.wait_recv()
    cut(here.row[1])
    cut(here.corner[1])
    project(x_ref, lambda: rows_of(chans, 2 * chans))
    second.forward()
    third = Relay(lambda i: wo_g.at[i, x])
    third.begin()
    bc_core_copy.wait_recv()
    turn(bc_g, 2 * chans)
    project(bc_ref, lambda: rows_of(2 * chans, 2 * chans + 4 * state))
    project(pre_ref, lambda: halves(dtt[...] * gain_row[...]))
    c_copies[0].wait_recv()
    c_far = links.copy(cq.at[other], cq.at[other], here.core)
    convolve(x_ref, bc_ref, live_ref, cx_ref, cbc_ref, xc, dx_act, b_s, c_s, dbc_act)
    second.wait()
    third.forward()
    step_sizes(pre_ref, hp_ref, step_s, cum_s, cumex_s, heads)
    states(xc, b_s, step_s, cum_s, dh_s, hcat, heads)
    turn(wz_g, 0)
    project(z_ref, lambda: rows_of(0, chans))

    def stat_copy(j, b):
        return pltpu.make_async_remote_copy(
            src_ref=stat_own.at[b],
            dst_ref=stat_g.at[n, b],
            send_sem=stat_send.at[j, b],
            recv_sem=stat_recv.at[j, b],
            device_id=group[j],
            device_id_type=MESH,
        )

    def tell(b, row):
        stats = jnp.broadcast_to(row, (8, SPAN))
        stat_own[b] = stats
        stat_g[n, b] = stats
        for j in range(3):
            stat_copy(j, b).start()

    def told(b):
        for j in range(3):
            stat_copy(j, b).wait_recv()
        total = stat_g[0, b]
        for q in range(1, parts):
            total = total + stat_g[q, b]
        return total[0:1]

    def emit(b, sl, h, rows, gated, sums):
        onorm[rows, sl] = gated
        row = jnp.sum(gated * gated, axis=0, keepdims=True)
        row = row if sums is None else row + sums
        if h == heads - 1:
            tell(b, row)
        return row

    outputs(z_ref, xc, b_s, c_s, step_s, cum_s, cumex_s, hcat, hp_ref, y_s, inner_s, heads, emit)
    rms = jnp.concatenate(
        [lax.rsqrt(told(b) / inner_total + 1e-05) for b in range(blocks)], axis=1
    )

    def scale_rows(i, _):
        rows = pl.ds(pl.multiple_of(i * 8, 8), 8)
        onorm[rows, :] = onorm[rows, :] * rms * og_ref[rows, :]
        return 0

    lax.fori_loop(0, chans // 8, scale_rows, 0, unroll=2)
    c_copies[1].wait_recv()
    c_far.wait_recv()

    def weight_grad(put, right, left=lambda q: (hq_hi[q], hq_lo[q])):
        def body(q):
            put(q, product(left(q), halves(right(q)), NT))

        each_quarter(body)

    block_shape = part.shape[1:]

    def add_to(start, count):
        def put(q, value):
            for i in range(count):
                ref = part.at[start + i]
                piece = value[:, i * 128 : (i + 1) * 128].reshape(block_shape)
                ref[...] = jnp.where(q == 0, piece, ref[...] + piece)

        return put

    def scaled(i):
        part[i] = (flat(part[i]) * gain_col[...]).reshape(block_shape)

    part[...] = jnp.zeros_like(part)
    for start, stop in ((0, 1), (1, thirds)):
        rows = slice(start * 128, stop * 128)
        weight_grad(
            add_to(thirds + start, stop - start),
            lambda q, rows=rows: onorm[rows, quarter(q)],
            lambda q: halves(cq[q]),
        )
        for job in o_jobs[start:stop]:
            job.start()
    third.wait()
    turn(wo_g, 0, False)

    def donorm(q):
        don[:, quarter(q)] = product(rows_of(0, chans), halves(cq[q]))

    each_quarter(donorm)

    def inner_sums(b, _):
        sl = pl.ds(pl.multiple_of(b * SPAN, SPAN), SPAN)
        gate = z_ref[:, sl]
        gated = y_s[:, sl] * (gate * sigmoid(gate))
        tell(blocks + b, jnp.sum(gated * (don[:, sl] * og_ref[...]), axis=0, keepdims=True))
        return 0

    lax.fori_loop(0, blocks, inner_sums, 0)

    links.release(c_copies + [c_far])

    class Return:
        def __init__(self, rx, row_rx, compute, steps=((), (), (), ())):
            self.rx, self.row_rx = rx, row_rx
            first = links.count
            self.cores = [links.plan(cq.at[k * 2 + 1 - c], rx.at[k], here.core) for k in range(2)]
            self.last = links.plan(rx.at[1 - y], row_rx, here.row)

            def body(k, _):
                q = (k % 2) * 2 + (c + 1 + k // 2) % 2
                cq[q] = compute(q)

                @pl.when(k < 2)
                def _():
                    pltpu.make_async_remote_copy(
                        src_ref=cq.at[q],
                        dst_ref=rx.at[k % 2],
                        send_sem=links.send.at[first + k % 2],
                        recv_sem=links.recv.at[first + k % 2],
                        device_id=here.core,
                        device_id_type=MESH,
                    ).start()

                for at, items in enumerate(steps):

                    @pl.when(k == at)
                    def _(items=items):
                        for step in items:
                            step()

                return 0

            lax.fori_loop(0, 4, body, 0)

        def fold(self):
            arrived(self.cores)
            for k in range(2):
                self.rx[k] = self.rx[k] + cq[k * 2 + c]
            self.last.start()

        def total(self):
            self.last.wait_recv()
            return self.rx[y] + self.row_rx[...]

    o0, o1, o2 = o_jobs
    z0, z1, z2 = z_jobs
    x0, x1, x2 = x_jobs
    branch = Return(core_rx.at[0], row_rx.at[0], lambda q: dot3(flat(wo_g[...]), onorm[:, quarter(q)]))
    o0.fold()
    told_inner = jnp.concatenate([told(blocks + b) for b in range(blocks)], axis=1)
    coef = rms**3 * told_inner / inner_total
    gate_back(z_ref, y_s, don, rms, coef, og_ref, dy_s, z_ref, dog_s)
    weight_grad(add_to(0, thirds), lambda q: z_ref[:, quarter(q)])
    for i, job in enumerate(z_jobs):
        scaled(i)
        job.start()
    o1.fold()
    o0.own()

    def x_grad(i):
        links.release([o_jobs[i].first])
        part[thirds + i] = jnp.zeros(block_shape, F32)
        weight_grad(add_to(thirds + i, 1), lambda q: x_ref[i * 128 : (i + 1) * 128, quarter(q)])
        scaled(thirds + i)

    within = [
        {0: [o2.fold], 6: [o1.own, z0.fold]},
        {1: [o2.own, z2.fold], 3: [branch.fold], 5: [o1.spread]},
        {0: [z1.own], 5: [o2.spread], 6: [x1.fold]},
    ]
    between = [
        {6: [o0.spread], 7: [z1.fold]},
        {6: [z0.own, x0.fold]},
        {4: [z2.own]},
    ]

    def ticks(plan):
        def tick(b):
            for at, steps in plan.items():

                @pl.when(b == at)
                def _(steps=steps):
                    for step in steps:
                        step()

        return tick

    for i, chosen in enumerate(pairs_of(heads)):
        back_intra(
            xc, c_s, inner_s, step_s, cum_s, cumex_s, hcat, hp_ref, dy_s, y_s, dh_s, dc_s,
            din_s, g_s, cv_s, dd_s, chosen, heads, ticks(within[i]),
        )
        back_states(cum_s, hcat, dh_s, tq_s, state, chosen, heads)
        back_inter(xc, b_s, step_s, cum_s, y_s, dh_s, db_s, v_s, chosen, heads, ticks(between[i]))
        conv_x_back(x_ref, cx_ref, dx_act, y_s, x_ref, cols_s, i * 128, 128)
        x_grad(i)
        x_jobs[i].start()

    back_logs(
        b_s, c_s, pre_ref, step_s, hp_ref, pre_ref, dhp_s, db_s, dc_s, din_s, g_s, cv_s, v_s, dd_s, tq_s, heads
    )
    z0.spread()
    conv_bc_back(bc_ref, cbc_ref, dbc_act, db_s, dc_s, bc_ref, dcbc_s)
    gbc_shape = gbc.shape

    def add_bc(q, value):
        gbc[...] = jnp.where(q == 0, value.reshape(gbc_shape), gbc[...] + value.reshape(gbc_shape))

    gbc[...] = jnp.zeros_like(gbc)
    weight_grad(add_bc, lambda q: bc_ref[:, quarter(q)])
    gbc[...] = (flat(gbc[...]) * gain_col[...]).reshape(gbc_shape)
    bc_first = links.copy(gbc.at[:, :, 1 - c], bc_core, here.core)
    x0.own()
    x2.fold()
    dt_grad = jnp.zeros((16, width), F32)
    for q in range(parts):
        step = halves(pre_ref[:, q * own_rows : (q + 1) * own_rows])
        dt_grad = dt_grad + product(step, (hq_hi[q], hq_lo[q]), NT)
    dt_grad = dt_grad * gain_row[...]
    gdt[...] = jnp.zeros_like(gdt)
    for i in range(wide):
        gdt[i, :, 0:lanes] = dt_grad[:, i * lanes : (i + 1) * lanes]
    dt_rx[w] = gdt[w]
    dt_copies = [links.copy(gdt.at[device[0]], dt_rx.at[w], device) for device in far]
    dgain_s[...] = jnp.zeros_like(dgain_s)
    bc_first.wait_recv()
    for k in range(2):
        bc_core[:, k] = bc_core[:, k] + gbc[:, k, c]
    for k in range(wide):
        bc_mine[k] = bc_core[k, 1 - y]
    bc_second = links.copy(bc_mine, bc_row, here.row)

    links.release(branch.cores)

    for k in range(parts):
        pieces_of = []
        for ref, start in ((wz_g, 0), (wx_g, chans), (bc_g, 2 * chans)):
            a, b = max(k * own_rows, start), min((k + 1) * own_rows, start + ref.shape[-1])
            if a < b:
                pieces_of.append(flat(ref[..., a - start : b - start]))
        hq_hi[k], hq_lo[k] = halves(jnp.concatenate(pieces_of, axis=1))

    def normed_back(q):
        sl = quarter(q)

        def add(k, value):
            rows = pl.ds(pl.multiple_of(k * own_rows, 8), own_rows)
            return value + product((hq_hi[k], hq_lo[k]), halves(proj[rows, sl]))

        value = lax.fori_loop(0, parts, add, dot3(dtt[...], pre_ref[:, sl], TN))
        dgain_s[...] = dgain_s[...] + jnp.sum(value * hq[q], axis=1, keepdims=True)
        return value

    back = Return(core_rx.at[1], row_rx.at[1], normed_back, ([z1.spread], [], [x1.own], []))
    back.fold()
    small = 128
    shared_g[n] = jnp.zeros(shared_g.shape[1:], F32)
    for i in range(4 * state // 128):
        sl = slice(i * 128, (i + 1) * 128)
        shared_g[n, 0:4, sl] = jnp.transpose(dcbc_s[sl, :])[0:4]
    for i in range(width // 128):
        shared_g[n, 8 + i : 9 + i, 0:128] = as_row(dgain_s[i * 128 : (i + 1) * 128, :])
    shared_copies = [links.copy(shared_g.at[n], shared_g.at[n], device) for device in group]
    bc_second.wait_recv()
    links.release([bc_second])
    for k in range(wide):
        bc_mine[k] = bc_core[k, y] + bc_row[k]
    bc_rx[w] = bc_mine[w]
    bc_copies = [links.copy(bc_mine.at[device[0]], bc_rx.at[w], device) for device in far]
    sv_g[w] = jnp.zeros(sv_g.shape[1:], F32)
    for i in range(thirds):
        sl = slice(i * 128, (i + 1) * 128)
        sv_g[w, 0:4, sl] = jnp.transpose(cols_s[sl, :])[0:4]
        sv_g[w, 4:5, sl] = as_row(dog_s[sl, :])
    sv_g[w, :, chans : chans + small] = dhp_s[...]
    z2.spread()
    arrived(shared_copies)
    total = shared_g[0]
    for q in range(1, parts):
        total = total + shared_g[q]
    sv_g[w, :, chans + small :] = total
    sv_copies = [links.copy(sv_g.at[w], sv_g.at[w], device) for device in far]

    arrived(bc_copies)
    own = bc_rx[0]
    for k in range(1, wide):
        own = own + bc_rx[k]
    bc_own[n] = own
    bc_group = [links.copy(bc_own.at[n], bc_own.at[n], device) for device in group]
    squares = total_square(own)
    arrived(dt_copies)
    own = dt_rx[0]
    for k in range(1, wide):
        own = own + dt_rx[k]
    dt_own[...] = own
    squares = squares + total_square(own)
    arrived(sv_copies)
    own = sv_g[0]
    for k in range(1, wide):
        own = own + sv_g[k]
    sv_sum[...] = own
    x0.spread()
    x2.own()
    for i in range(3 * thirds):
        squares = squares + square_s[i][:, 0:1]
    once = jnp.where(w == 0, 1.0, 0.0)
    squares = squares + once * total_square(own[:, 0 : chans + small])
    squares = squares + jnp.where(n == 0, once, 0.0) * total_square(own[:, chans + small :])
    norm_n[n] = jnp.broadcast_to(squares, (8, 128))
    norm_copies = [links.copy(norm_n.at[n], norm_n.at[n], device) for device in group]

    x1.spread()

    block = branch.total() * live_ref[:, pl.ds(pl.multiple_of(n * own_rows, 128), own_rows)]
    for i in range(width // 128):
        sl = slice(i * 128, (i + 1) * 128)
        block_ref[:, sl] = hidden_ref[:, sl] + jnp.transpose(block[sl, :])
    arrived(norm_copies)
    norm_w[w] = norm_n[0] + norm_n[1] + norm_n[2] + norm_n[3]
    wide_copies = [links.copy(norm_w.at[w], norm_w.at[w], device) for device in far]
    x2.spread()
    dn = back.total() * gain_col[...]
    dots = jnp.sum(dn * hq[n], axis=0, keepdims=True) / width
    for i in range(width // 128):
        sl = slice(i * 128, (i + 1) * 128)
        value = inv_ref[...] * (dn[sl] - hq[n, sl, :] * dots)
        grad_ref[:, sl] = cot_ref[:, sl] + jnp.transpose(value)
    arrived(wide_copies)
    total = norm_w[0]
    for k in range(1, wide):
        total = total + norm_w[k]
    norm_ref[...] = jnp.sqrt(total)
    for job in jobs:
        job.finish()
    arrived(bc_group)
    links.drain()

    def sent(b, _):
        for j in range(3):
            stat_copy(j, b).wait_send()
        return 0

    lax.fori_loop(0, 2 * blocks, sent, 0)


def run_layer(lengths, hidden, cot, gain, w_zx, w_out, w_bc, dtw, cx, cbc, hp, og, heads, shard, wide, narrow):
    own_rows, width = hidden.shape
    tokens = own_rows * narrow
    chans, n4 = cx.shape[1], cbc.shape[1]
    rows = w_zx.shape[1]
    depth, blocks, half, thirds = wide // 2, tokens // SPAN, n4 // 2, chans // 128
    full, bc2, small = (chans, tokens), (half, tokens), (16, tokens)
    quarters = (narrow, width, own_rows)
    weights = (depth, 2, rows, chans)
    piece = (3 * thirds, depth, 2, rows, 128)
    quarter = (width // wide // 4, n4)
    sums = (16, chans + 128 + 256)
    shapes = [
        hidden.shape,
        hidden.shape,
        piece,
        (4,) + quarter,
        (16, 128),
        sums,
        (8, 128),
    ]
    scratch = [
        quarters,
        quarters,
        weights,
        weights,
        weights,
        (depth, 2, 2, rows // 2, n4),
        (depth, 2, 16, 128),
        (narrow, 8, 128),
        (16, width),
        (width, 1),
        (1, width),
        (128, 128),
        (chans, 4),
        (n4, 4),
        (16, 3),
        (chans, 1),
        (1, tokens),
        (1, own_rows),
        (2 * chans + n4 + 16, tokens),
        full,
        full,
        full,
        bc2,
        bc2,
        (n4, tokens),
        small,
        small,
        small,
        (blocks, chans, half),
        (blocks, SPAN, SPAN),
        full,
        full,
        full,
        (blocks, chans, half),
        bc2,
        bc2,
        (blocks, SPAN, SPAN),
        small,
        small,
        small,
        small,
        (blocks, 16, SPAN),
        (chans, 128),
        (n4, 128),
        (16, 128),
        (chans, 1),
        (width, 1),
        (2 * blocks, 8, 128),
        (narrow, 2 * blocks, 8, 128),
        (2 * thirds,) + piece[1:],
        (3 * thirds, depth, rows, 128),
        (3 * thirds, depth - 1, rows, 128),
        (2, 2, width, own_rows),
        (2, width, own_rows),
        (wide, 2, 2) + quarter,
        (wide, 2) + quarter,
        (wide,) + quarter,
        (wide,) + quarter,
        (wide,) + quarter,
        (wide, 16, 128),
        (wide, 16, 128),
        (narrow, 16, 256),
        (wide,) + sums,
        (narrow, 8, 128),
        (wide, 8, 128),
        (3 * thirds, 1, 128),
    ]
    lows = [quarters] * 2 + [(2 * chans + n4, width)] * 2
    copies = 200
    operands = (lengths, hidden, cot, gain, w_zx, w_out, w_bc, dtw, cx, cbc, hp, og)
    return pl.pallas_call(
        functools.partial(layer_kernel, wide, heads, shard, chans * narrow),
        out_shape=[jax.ShapeDtypeStruct(shape, F32) for shape in shapes],
        in_specs=[pl.BlockSpec(memory_space=pltpu.SMEM)]
        + [pl.BlockSpec(memory_space=pltpu.VMEM)] * (len(operands) - 1),
        scratch_shapes=[pltpu.VMEM(shape, F32) for shape in scratch]
        + [pltpu.VMEM(shape, jnp.bfloat16) for shape in lows]
        + [
            pltpu.SemaphoreType.DMA((copies,)),
            pltpu.SemaphoreType.DMA((copies,)),
            pltpu.SemaphoreType.DMA((3, 2 * blocks)),
            pltpu.SemaphoreType.DMA((3, 2 * blocks)),
        ],
        compiler_params=pltpu.CompilerParams(
            vmem_limit_bytes=62 * MIB, collective_id=0, has_side_effects=True
        ),
        cost_estimate=pl.CostEstimate(flops=20_000_000_000, bytes_accessed=20_000_000, transcendentals=0),
    )(*operands)


def finish_kernel(
    wide,
    narrow,
    gfull,
    bc_own,
    dt_own,
    sv,
    norm_ref,
    block_in,
    grad_in,
    stat_l,
    stat_r,
    stat_lo,
    stat_ro,
    root_l,
    root_r,
    root_lo,
    root_ro,
    w_ref,
    wout_ref,
    bcw_ref,
    dtw_ref,
    cx_ref,
    cbc_ref,
    hp_ref,
    og_ref,
    gain_ref,
    block_out,
    in_grad,
    clip,
    g_zx,
    new_zx,
    new_l,
    new_r,
    g_out,
    new_out,
    new_lo,
    new_ro,
    g_bc,
    new_bc,
    g_dt,
    new_dt,
    g_cx,
    new_cx,
    g_cbc,
    new_cbc,
    g_hp,
    new_hp,
    g_og,
    new_og,
    g_ng,
    new_ng,
    g_s,
    l_s,
    r_s,
    lo_s,
    ro_s,
    rl_s,
    rr_s,
    rlo_s,
    rro_s,
    in_sem,
    out_sem,
):
    rate = 10.0
    chans = w_ref.shape[2]
    thirds = chans // 128
    place = lax.axis_index("wide")
    z, x = place // 2, place % 2
    factor = 1.0 / jnp.maximum(norm_ref[0:1, 0:1], 1.0)
    fetches, results = [], []

    def fetch(src, dst):
        item = pltpu.make_async_copy(src, dst, in_sem.at[len(fetches)])
        item.start()
        fetches.append(item)
        return item

    def result(src, dst):
        item = pltpu.make_async_copy(src, dst, out_sem.at[len(results)])
        item.start()
        results.append(item)

    waits = []
    for m in (2, 0, 1):
        gs = g_s.at[m * thirds : (m + 1) * thirds]
        whole_m = fetch(gfull.at[m * thirds : (m + 1) * thirds], gs)
        if m == 2:
            others = [(root_ro, rro_s), (root_lo, rlo_s), (stat_ro, ro_s), (stat_lo, lo_s)]
        else:
            others = [(root_l.at[m], rl_s.at[m]), (root_r.at[m], rr_s.at[m])]
            others += [(stat_l.at[m], l_s.at[m]), (stat_r.at[m], r_s.at[m])]
        waits.append([whole_m] + [fetch(*pair) for pair in others])
    block_out[...] = block_in[...]
    in_grad[...] = grad_in[...]
    clip[...] = norm_ref[0:1, 0:1]

    def both(m):
        for item in waits[(1, 2, 0)[m]]:
            item.wait()
        parts = [flat(g_s[m * thirds + i]) for i in range(thirds)]
        mine = [g_s[m * thirds + i, z, x] for i in range(thirds)]
        return jnp.concatenate(mine, axis=1) * factor, halves(jnp.concatenate(parts, axis=1) * factor)

    own, full = both(2)
    g_out[...] = own
    ro_s[...] = 0.5 * ro_s[...] + 0.5 * product(halves(own), full, NT)
    result(ro_s, new_ro)
    lo_s[...] = 0.5 * lo_s[...] + 0.5 * product(full, full, TN)
    result(lo_s, new_lo)
    new_out[...] = wout_ref[...] - 0.5 * dot3(product(halves(rro_s[...]), full), rlo_s[...], NT)
    for m in range(2):
        own, full = both(m)
        g_zx[m] = own
        l_s[m] = 0.5 * l_s[m] + 0.5 * product(halves(own), full, NT)
        result(l_s.at[m], new_l.at[m])
        r_s[m] = 0.5 * r_s[m] + 0.5 * product(full, full, TN)
        result(r_s.at[m], new_r.at[m])
        new_zx[m] = w_ref[m] - 0.5 * dot3(product(halves(rl_s[m]), full), rr_s[m])

    grad = flat(bc_own[...]) * factor
    g_bc[...] = grad
    new_bc[...] = bcw_ref[...] - rate * grad
    heads, _, rows = dtw_ref.shape
    for h in range(heads):
        for i in range(2):
            row = i * heads + h
            grad = dt_own[row : row + 1, 0:rows] * factor
            g_dt[h, i : i + 1, :] = grad
            new_dt[h, i : i + 1, :] = dtw_ref[h, i : i + 1, :] - rate * grad
    sums = sv[...] * factor
    grad = sums[0:4, 0:chans]
    g_cx[...] = grad
    new_cx[...] = cx_ref[...] - rate * grad
    grad = sums[4:5, 0:chans]
    g_og[...] = grad.reshape(chans)
    new_og[...] = og_ref[...] - rate * g_og[...]
    n4 = cbc_ref.shape[1]
    last = chans + 128
    grad = sums[0:4, last : last + n4]
    g_cbc[...] = grad
    new_cbc[...] = cbc_ref[...] - rate * grad
    turned = jnp.transpose(
        jnp.concatenate([sums[:, chans:last], jnp.zeros((112, 128), F32)], axis=0)
    )
    for i, (row, start) in enumerate(((0, 0), (0, heads), (1, 0), (1, heads), (2, 0))):
        grad = turned[row : row + 1, start : start + heads]
        g_hp[i : i + 1, :] = grad
        new_hp[i : i + 1, :] = hp_ref[i : i + 1, :] - rate * grad
    shard = gain_ref.shape[0]
    count = narrow * shard // 128
    line = jnp.concatenate([sums[8 + i : 9 + i, last : last + 128] for i in range(count)], axis=1)
    grad = jnp.zeros((1, shard), F32)
    for q in range(narrow):
        piece = line[:, q * shard : (q + 1) * shard]
        grad = jnp.where(lax.axis_index("narrow") == q, piece, grad)
    g_ng[...] = grad.reshape(shard)
    new_ng[...] = gain_ref[...] - rate * g_ng[...]
    for item in results:
        item.wait()


def run_finish(partials, stats, roots, params, tokens_shape, wide, narrow):
    stat_l, stat_r, stat_lo, stat_ro = stats
    w_zx, w_out, w_bc, w_dt, cx, cbc, hp, og, gain = params
    like = [w_zx, w_zx, stat_l, stat_r, w_out, w_out, stat_lo, stat_ro]
    like += [item for item in (w_bc, w_dt, cx, cbc, hp, og, gain) for _ in range(2)]
    shapes = [tokens_shape, tokens_shape, (1, 1)] + [item.shape for item in like]
    far, near = pl.BlockSpec(memory_space=pl.ANY), pl.BlockSpec(memory_space=pltpu.VMEM)
    gfull = partials[0]
    kept = [gfull, stat_l, stat_r, stat_lo, stat_ro, *roots]
    return pl.pallas_call(
        functools.partial(finish_kernel, wide, narrow),
        out_shape=[jax.ShapeDtypeStruct(shape, F32) for shape in shapes],
        in_specs=[far] + [near] * 6 + [far] * 8 + [near] * len(params),
        out_specs=[near] * 5 + [far] * 2 + [near] * 2 + [far] * 2 + [near] * (len(shapes) - 11),
        scratch_shapes=[pltpu.VMEM(item.shape, F32) for item in kept]
        + [pltpu.SemaphoreType.DMA((15,)), pltpu.SemaphoreType.DMA((6,))],
        compiler_params=pltpu.CompilerParams(vmem_limit_bytes=56 * MIB),
        cost_estimate=pl.CostEstimate(flops=4_000_000_000, bytes_accessed=20_000_000, transcendentals=0),
    )(*partials, *stats, *roots, *params)


def fast_local(
    wide,
    narrow,
    hidden_in,
    out_cot,
    lengths,
    norm_gain,
    w_zx,
    w_bc,
    w_dt,
    conv_x,
    conv_bc,
    head_params,
    out_gain,
    w_out,
    left_statistic_gate,
    stat_right_zx,
    stat_left_out,
    stat_right_out,
    inverse_root_left_gate,
    inverse_root_right_gate,
    root_left_out,
    root_right_out,
):
    heads, shard = w_dt.shape[1], norm_gain.shape[0]
    out_rows, dt_rows = w_out.T, jnp.transpose(w_dt, (1, 2, 0))
    block, grad, *partials = run_layer(
        lengths,
        hidden_in,
        out_cot,
        norm_gain,
        w_zx,
        out_rows,
        w_bc,
        dt_rows,
        conv_x,
        conv_bc,
        head_params,
        out_gain,
        heads,
        shard,
        wide,
        narrow,
    )
    (
        block_out,
        in_grad,
        clip,
        g_zx,
        new_zx,
        new_l,
        new_r,
        g_out,
        new_out,
        new_lo,
        new_ro,
        g_bc,
        new_bc,
        g_dt,
        new_dt,
        *rest,
    ) = run_finish(
        (*partials, block, grad),
        (left_statistic_gate[:, 0], stat_right_zx, stat_left_out, stat_right_out[0]),
        (inverse_root_left_gate[:, 0], inverse_root_right_gate, root_left_out, root_right_out[0]),
        (w_zx, out_rows, w_bc, dt_rows, conv_x, conv_bc, head_params, out_gain, norm_gain),
        hidden_in.shape,
        wide,
        narrow,
    )
    return (
        block_out,
        in_grad,
        clip.reshape(()),
        g_zx,
        new_zx,
        new_l[:, None],
        new_r,
        g_out.T,
        new_out.T,
        new_lo,
        new_ro[None],
        g_bc,
        new_bc,
        jnp.transpose(g_dt, (2, 0, 1)),
        jnp.transpose(new_dt, (2, 0, 1)),
        *rest,
    )


def solution(mesh):
    wide, narrow = mesh.shape["wide"], mesh.shape["narrow"]
    body = functools.partial(fast_local, wide, narrow) if (wide, narrow) == (8, 4) else local
    return jax.shard_map(
        body,
        mesh=mesh,
        in_specs=(
            P(("wide", "narrow"), None),
            P(("wide", "narrow"), None),
            P("wide"),
            P("narrow"),
            P(None, "wide", "narrow"),
            P("wide", None),
            P("wide", "narrow", None),
            P(None, "narrow"),
            P(),
            P(None, "narrow"),
            P("narrow"),
            P("narrow", "wide"),
            P(None, "narrow", "wide", None),
            P(None, "narrow", None),
            P("narrow", None),
            P("narrow", "wide", None),
            P(None, "narrow", "wide", None),
            P(None, "narrow", None),
            P("narrow", None),
            P("narrow", "wide", None),
        ),
        out_specs=(
            P(("wide", "narrow"), None),
            P(("wide", "narrow"), None),
            P(),
            P(None, "wide", "narrow"),
            P(None, "wide", "narrow"),
            P(None, "narrow", "wide", None),
            P(None, "narrow", None),
            P("narrow", "wide"),
            P("narrow", "wide"),
            P("narrow", None),
            P("narrow", "wide", None),
            P("wide", None),
            P("wide", None),
            P("wide", "narrow", None),
            P("wide", "narrow", None),
            P(None, "narrow"),
            P(None, "narrow"),
            P(),
            P(),
            P(None, "narrow"),
            P(None, "narrow"),
            P("narrow"),
            P("narrow"),
            P("narrow"),
            P("narrow"),
        ),
        check_vma=False,
    )
```

time: 1060 us -> 232 us (0.22)
  waiting for transfers between devices: 276 us -> 0 us
  local copies, waits for them, and re-layouts: 244 us -> 0 us
  Pallas kernels: 0 us -> 228 us
  matrix products: 205 us -> 0 us
  blocking collectives: 178 us -> 0 us
  other arithmetic: 121 us -> 0 us
  between operations: 25.6 us -> 1.52 us
    pallas_call x0 -> x2, Pallas kernels: none -> 228 us  [the longest x1 215 us: run_layer(): pl.pallas_call(functools.partial(layer_kernel, wide, heads, shard, chans...]
    psum x3 -> x0, waiting for transfers between devices: 208 us -> none  [the longest x1 98 us: local(): lax.psum((d_zx, grad_out, d_dt, d_convx, d_head, grad_ogain, grad_ngain),...]
    dot_general x47 -> x0, matrix products: 205 us -> none  [the longest x6 40.2 us: scan_ssd(): jnp.einsum('schtu,schup->schtp', weights, xq, precision=hyper_parameters)]
    psum x5 -> x0, blocking collectives: 99.6 us -> none  [the longest x1 40.4 us: local(): g_bc, g_cbc = lax.psum((d_bc, d_convbc), ('wide', 'narrow'))]
    all_gather x2 -> x0, blocking collectives: 69.7 us -> none  [the longest x1 36 us: local(): lax.all_gather(w_bc, 'wide', axis=0, tiled=True)]
    reduce_sum x35 -> x0, other arithmetic: 49.3 us -> none  [the longest x16 18 us: advance(): return (carry * factor[..., None, None] + piece, carry)]
    unnamed x352 -> x0, local copies, waits for them, and re-layouts: 49.1 us -> none
    rev x11 -> x0, local copies, waits for them, and re-layouts: 49 us -> none  [the longest x2 25.7 us: mixer(): jnp.flip(xh, 1)]
  transfers between devices with their start and end apart: 8 -> 0, of which waited for: 5 -> 0; matrix products, arithmetic and copies ran while one was open for 22% -> 0% of each run, Pallas kernels for 0% -> 0%
where the time goes in v1:
time: 232 us; the launch traced here: 229 us
  Pallas kernels  228 us (98%)
    pallas_call x1, Pallas kernels, run_layer(): pl.pallas_call(functools.partial(layer_kernel, wide, heads, shard, chans...  215 us
    pallas_call x1, Pallas kernels, run_finish(): pl.pallas_call(functools.partial(finish_kernel, wide, narrow), out_shape=...  12.2 us

profile of v1, /device:TPU:0, one launch (start us, length us, event | category | flops | bytes accessed | tf_op | source)
XLA Modules:
  0.0 229.1 jit_solution(4539394397853327614)
XLA Ops:
  1.3 215.3 %shard_map.387 = (f32[256,768]{1,0:T(8,128)}, f32[256,768]{1,0:T(8,128)}, f32[9,4,2,96,128]{4,3,2,1,0:T(8,128)}, f32[4,24,256]{2,1,0:T(8,128)}, f32[16,128]{1,0:...) custom-call(s32[1]{0:T(128)S(6)} %copy.46.length_ref, f32[256,768]{1,0:T(8,128)} %hidden_ref.1, f32[256,768]{1,0:T(8,128)} %cot_ref.1, ...), custom_call_target="tpu_custom_call" | custom-call | flops 20000000000 | bytes 20000000 | tf_op jit(solution)/shard_map/pallas_call | solution.py:1652
  216.7 12.2 %shard_map.388 = (f32[256,768]{1,0:T(8,128)}, f32[256,768]{1,0:T(8,128)}, f32[1,1]{1,0:T(1,128)}, f32[2,96,384]{2,1,0:T(8,128)}, f32[2,96,384]{2,1,0:T(8,128)}, ...) custom-call(f32[9,4,2,96,128]{4,3,2,1,0:T(8,128)} %get-tuple-element, ...), custom_call_target="tpu_custom_call" | custom-call | flops 4000000000 | bytes 20000000 | tf_op jit(solution)/shard_map/pallas_call | solution.py:1843

commit v2 on v1

--- a/solution.py
+++ b/solution.py
@@ -29,12 +29,22 @@
 def product(a, b, dims=NN):
     (ah, al), (bh, bl) = a, b
     (left,), (right,) = dims[0]
-    return lax.dot_general(
-        jnp.concatenate([ah, al, ah], axis=left),
-        jnp.concatenate([bh, bh, bl], axis=right),
-        dims,
-        preferred_element_type=F32,
-    )
+    rows, depth = ah.shape[1 - left], ah.shape[left]
+
+    def times(u, v):
+        return lax.dot_general(u, v, dims, preferred_element_type=F32)
+
+    if depth < 128:
+        return times(
+            jnp.concatenate([ah, al, ah], axis=left), jnp.concatenate([bh, bh, bl], axis=right)
+        )
+    if depth == 128:
+        top = jnp.concatenate([ah, ah], axis=left)
+        low = jnp.concatenate([al, jnp.zeros_like(al)], axis=left)
+        out = times(jnp.concatenate([top, low], axis=1 - left), jnp.concatenate([bh, bl], axis=right))
+        return out[0:rows] + out[rows:]
+    out = times(jnp.concatenate([ah, al], axis=1 - left), bh)
+    return out[0:rows] + out[rows:] + times(ah, bl)
 
 
 def dot3(a, b, dims=NN):
@@ -1110,9 +1120,9 @@
 
     h_copies = exchange(hq.at[n])
     gain_copies = [links.copy(gain_g.at[n], gain_g.at[n], device) for device in group]
-    first = Relay(
-        lambda i: wx_g.at[i, x], lambda i: bc_g.at[i, x, c], lambda i: dt_g.at[i, x]
-    )
+    early = Relay(lambda i: bc_g.at[i, x, c], lambda i: dt_g.at[i, x])
+    early.begin()
+    first = Relay(lambda i: wx_g.at[i, x])
     first.begin()
 
     wz_g[z, x] = w_ref[0]
@@ -1146,6 +1156,7 @@
     cut(n)
     h_copies[1].wait_recv()
     cut(here.core[1])
+    early.forward()
     first.forward()
     second = Relay(lambda i: wz_g.at[i, x])
     h_copies[0].wait_recv()
@@ -1189,24 +1200,25 @@
 
         each_quarter(body)
 
-    first.wait()
-    second.begin()
+    early.wait()
     bc_core_copy = links.copy(bc_g.at[:, :, c], bc_g.at[:, :, c], here.core)
-    turn(wx_g, chans)
     lanes = width // wide
     for i in range(wide):
         dtt[:, i * lanes : (i + 1) * lanes] = dt_g[i // 2, i % 2][:, 0:lanes]
+    last = 2 * chans + 4 * state
+    wt_hi[last:, :], wt_lo[last:, :] = halves(dtt[...] * gain_row[...])
+    bc_core_copy.wait_recv()
+    turn(bc_g, 2 * chans)
+    first.wait()
+    second.begin()
+    turn(wx_g, chans)
     h_far.wait_recv()
     cut(here.row[1])
     cut(here.corner[1])
-    project(x_ref, lambda: rows_of(chans, 2 * chans))
+    project(proj.at[chans:], lambda: rows_of(chans, last + 16))
     second.forward()
     third = Relay(lambda i: wo_g.at[i, x])
     third.begin()
-    bc_core_copy.wait_recv()
-    turn(bc_g, 2 * chans)
-    project(bc_ref, lambda: rows_of(2 * chans, 2 * chans + 4 * state))
-    project(pre_ref, lambda: halves(dtt[...] * gain_row[...]))
     c_copies[0].wait_recv()
     c_far = links.copy(cq.at[other], cq.at[other], here.core)
     convolve(x_ref, bc_ref, live_ref, cx_ref, cbc_ref, xc, dx_act, b_s, c_s, dbc_act)
@@ -1646,7 +1658,7 @@
         (wide, 8, 128),
         (3 * thirds, 1, 128),
     ]
-    lows = [quarters] * 2 + [(2 * chans + n4, width)] * 2
+    lows = [quarters] * 2 + [(2 * chans + n4 + 16, width)] * 2
     copies = 200
     operands = (lengths, hidden, cot, gain, w_zx, w_out, w_bc, dtw, cx, cbc, hp, og)
     return pl.pallas_call(

time: 232 us -> 229 us (0.987)
  Pallas kernels: 228 us -> 225 us
where the time goes in v2:
time: 229 us; the launch traced here: 226 us
  Pallas kernels  225 us (98%)
    pallas_call x1, Pallas kernels, run_layer(): pl.pallas_call(functools.partial(layer_kernel, wide, heads, shard, chans...  213 us
    pallas_call x1, Pallas kernels, run_finish(): pl.pallas_call(functools.partial(finish_kernel, wide, narrow), out_shape=...  11.7 us

profile of v2, /device:TPU:0, one launch (start us, length us, event | category | flops | bytes accessed | tf_op | source)
XLA Modules:
  0.0 226.4 jit_solution(9374066487632988887)
XLA Ops:
  1.3 213.2 %shard_map.387 = (f32[256,768]{1,0:T(8,128)}, f32[256,768]{1,0:T(8,128)}, f32[9,4,2,96,128]{4,3,2,1,0:T(8,128)}, f32[4,24,256]{2,1,0:T(8,128)}, f32[16,128]{1,0:...) custom-call(s32[1]{0:T(128)S(6)} %copy.46.length_ref, f32[256,768]{1,0:T(8,128)} %hidden_ref.1, f32[256,768]{1,0:T(8,128)} %cot_ref.1, ...), custom_call_target="tpu_custom_call" | custom-call | flops 20000000000 | bytes 20000000 | tf_op jit(solution)/shard_map/pallas_call | solution.py:1664
  214.5 11.7 %shard_map.388 = (f32[256,768]{1,0:T(8,128)}, f32[256,768]{1,0:T(8,128)}, f32[1,1]{1,0:T(1,128)}, f32[2,96,384]{2,1,0:T(8,128)}, f32[2,96,384]{2,1,0:T(8,128)}, ...) custom-call(f32[9,4,2,96,128]{4,3,2,1,0:T(8,128)} %get-tuple-element, ...), custom_call_target="tpu_custom_call" | custom-call | flops 4000000000 | bytes 20000000 | tf_op jit(solution)/shard_map/pallas_call | solution.py:1855

commit v3 on v2

--- a/solution.py
+++ b/solution.py
@@ -1,4 +1,5 @@
 import functools
+import math
 
 import jax
 import jax.numpy as jnp
@@ -845,6 +846,35 @@
         return (self.w + k) % self.wide, self.n
 
 
+class Copy:
+    def __init__(self, src, dst, send, recv, device):
+        def piece(u, v):
+            return pltpu.make_async_remote_copy(
+                src_ref=u, dst_ref=v, send_sem=send, recv_sem=recv, device_id=device, device_id_type=MESH
+            )
+
+        shape = src.shape
+        unit = 8 if len(shape) == 2 else 1
+        count = max(1, round(4 * math.prod(shape) / 49152))
+        while shape[0] % (count * unit):
+            count -= 1
+        size = shape[0] // count
+        self.whole = piece(src, dst)
+        self.pieces = [
+            piece(src.at[i * size : (i + 1) * size], dst.at[i * size : (i + 1) * size]) for i in range(count)
+        ]
+
+    def start(self):
+        for item in self.pieces:
+            item.start()
+
+    def wait_recv(self):
+        self.whole.wait_recv()
+
+    def wait_send(self):
+        self.whole.wait_send()
+
+
 class Links:
     def __init__(self, send, recv):
         self.send, self.recv, self.count, self.started = send, recv, 0, []
@@ -852,14 +882,7 @@
     def plan(self, src, dst, device):
         i = self.count
         self.count = i + 1
-        item = pltpu.make_async_remote_copy(
-            src_ref=src,
-            dst_ref=dst,
-            send_sem=self.send.at[i],
-            recv_sem=self.recv.at[i],
-            device_id=device,
-            device_id_type=MESH,
-        )
+        item = Copy(src, dst, self.send.at[i], self.recv.at[i], device)
         self.started.append(item)
         return item
 
@@ -1338,14 +1361,8 @@
 
                 @pl.when(k < 2)
                 def _():
-                    pltpu.make_async_remote_copy(
-                        src_ref=cq.at[q],
-                        dst_ref=rx.at[k % 2],
-                        send_sem=links.send.at[first + k % 2],
-                        recv_sem=links.recv.at[first + k % 2],
-                        device_id=here.core,
-                        device_id_type=MESH,
-                    ).start()
+                    i = first + k % 2
+                    Copy(cq.at[q], rx.at[k % 2], links.send.at[i], links.recv.at[i], here.core).start()
 
                 for at, items in enumerate(steps):
 

time: 229 us -> 230 us (level)
  no operation moved by 1% of the time
where the time goes in v3:
time: 230 us; the launch traced here: 228 us
  Pallas kernels  226 us (98%)
    pallas_call x1, Pallas kernels, run_layer(): pl.pallas_call(functools.partial(layer_kernel, wide, heads, shard, chans...  214 us
    pallas_call x1, Pallas kernels, run_finish(): pl.pallas_call(functools.partial(finish_kernel, wide, narrow), out_shape=...  11.6 us

profile of v3, /device:TPU:0, one launch (start us, length us, event | category | flops | bytes accessed | tf_op | source)
XLA Modules:
  0.0 227.6 jit_solution(1968171046523880368)
XLA Ops:
  1.3 214.4 %shard_map.387 = (f32[256,768]{1,0:T(8,128)}, f32[256,768]{1,0:T(8,128)}, f32[9,4,2,96,128]{4,3,2,1,0:T(8,128)}, f32[4,24,256]{2,1,0:T(8,128)}, f32[16,128]{1,0:...) custom-call(s32[1]{0:T(128)S(6)} %copy.46.length_ref, f32[256,768]{1,0:T(8,128)} %hidden_ref.1, f32[256,768]{1,0:T(8,128)} %cot_ref.1, ...), custom_call_target="tpu_custom_call" | custom-call | flops 20000000000 | bytes 20000000 | tf_op jit(solution)/shard_map/pallas_call | solution.py:1681
  215.8 11.6 %shard_map.388 = (f32[256,768]{1,0:T(8,128)}, f32[256,768]{1,0:T(8,128)}, f32[1,1]{1,0:T(1,128)}, f32[2,96,384]{2,1,0:T(8,128)}, f32[2,96,384]{2,1,0:T(8,128)}, ...) custom-call(f32[9,4,2,96,128]{4,3,2,1,0:T(8,128)} %get-tuple-element, ...), custom_call_target="tpu_custom_call" | custom-call | flops 4000000000 | bytes 20000000 | tf_op jit(solution)/shard_map/pallas_call | solution.py:1872

commit v4 on v2

--- a/solution.py
+++ b/solution.py
@@ -1108,8 +1108,8 @@
         def begin(self):
             self.passed = [links.copy(view(z), view(z), here.across) for view in self.views]
 
-        def forward(self):
-            for k in range(1, depth):
+        def forward(self, steps=tuple(range(1, depth))):
+            for k in steps:
                 source = (z + depth - k) % depth
                 for view, copies in zip(self.views, self.direct):
                     copies[k - 1].wait_recv()
@@ -1211,23 +1211,25 @@
     turn(bc_g, 2 * chans)
     first.wait()
     second.begin()
+    second.forward((1,))
     turn(wx_g, chans)
+    second.forward((2,))
     h_far.wait_recv()
     cut(here.row[1])
     cut(here.corner[1])
     project(proj.at[chans:], lambda: rows_of(chans, last + 16))
-    second.forward()
+    second.forward((3,))
     third = Relay(lambda i: wo_g.at[i, x])
     third.begin()
     c_copies[0].wait_recv()
     c_far = links.copy(cq.at[other], cq.at[other], here.core)
     convolve(x_ref, bc_ref, live_ref, cx_ref, cbc_ref, xc, dx_act, b_s, c_s, dbc_act)
-    second.wait()
-    third.forward()
     step_sizes(pre_ref, hp_ref, step_s, cum_s, cumex_s, heads)
     states(xc, b_s, step_s, cum_s, dh_s, hcat, heads)
+    second.wait()
     turn(wz_g, 0)
     project(z_ref, lambda: rows_of(0, chans))
+    third.forward()
 
     def stat_copy(j, b):
         return pltpu.make_async_remote_copy(

time: 229 us -> 229 us (level)
  no operation moved by 1% of the time
where the time goes in v4:
time: 229 us; the launch traced here: 227 us
  Pallas kernels  225 us (98%)
    pallas_call x1, Pallas kernels, run_layer(): pl.pallas_call(functools.partial(layer_kernel, wide, heads, shard, chans...  214 us
    pallas_call x1, Pallas kernels, run_finish(): pl.pallas_call(functools.partial(finish_kernel, wide, narrow), out_shape=...  11.7 us

profile of v4, /device:TPU:0, one launch (start us, length us, event | category | flops | bytes accessed | tf_op | source)
XLA Modules:
  0.0 226.8 jit_solution(8186374506867592239)
XLA Ops:
  1.3 213.6 %shard_map.387 = (f32[256,768]{1,0:T(8,128)}, f32[256,768]{1,0:T(8,128)}, f32[9,4,2,96,128]{4,3,2,1,0:T(8,128)}, f32[4,24,256]{2,1,0:T(8,128)}, f32[16,128]{1,0:...) custom-call(s32[1]{0:T(128)S(6)} %copy.46.length_ref, f32[256,768]{1,0:T(8,128)} %hidden_ref.1, f32[256,768]{1,0:T(8,128)} %cot_ref.1, ...), custom_call_target="tpu_custom_call" | custom-call | flops 20000000000 | bytes 20000000 | tf_op jit(solution)/shard_map/pallas_call | solution.py:1666
  215.0 11.7 %shard_map.388 = (f32[256,768]{1,0:T(8,128)}, f32[256,768]{1,0:T(8,128)}, f32[1,1]{1,0:T(1,128)}, f32[2,96,384]{2,1,0:T(8,128)}, f32[2,96,384]{2,1,0:T(8,128)}, ...) custom-call(f32[9,4,2,96,128]{4,3,2,1,0:T(8,128)} %get-tuple-element, ...), custom_call_target="tpu_custom_call" | custom-call | flops 4000000000 | bytes 20000000 | tf_op jit(solution)/shard_map/pallas_call | solution.py:1857

commit v5 on v4

--- a/solution.py
+++ b/solution.py
@@ -918,6 +918,7 @@
         ]
         self.third = [links.plan(place, place, here.along(k)) for k in steps]
         self.fourth = links.plan(column, column, here.across)
+        self.holding = [self.first]
 
     def start(self):
         self.first.start()
@@ -943,6 +944,46 @@
 
     def finish(self):
         self.fourth.wait_recv()
+
+
+class CrossPiece:
+    def __init__(self, here, links, part, z_rx, x_rx, full, square):
+        self.here, self.part, self.z_rx, self.x_rx = here, part, z_rx, x_rx
+        self.full, self.square = full, square
+        steps = range(1, here.depth)
+        mine, pair = full.at[here.z, here.x], full.at[here.z]
+        self.first = [
+            links.plan(part.at[(here.z + k) % here.depth], z_rx.at[k - 1], here.along(k)) for k in steps
+        ]
+        self.second = links.plan(part.at[here.z, 1 - here.x], x_rx, here.across)
+        self.third = links.plan(mine, mine, here.across)
+        self.fourth = [links.plan(pair, pair, here.along(k)) for k in steps]
+        self.holding = [*self.first, self.second]
+
+    def start(self):
+        begin(self.first)
+
+    def fold(self):
+        arrived(self.first)
+        total = self.part[self.here.z]
+        for k in range(1, self.here.depth):
+            total = total + self.z_rx[k - 1]
+        self.part[self.here.z] = total
+        self.second.start()
+
+    def own(self):
+        self.second.wait_recv()
+        total = self.part[self.here.z, self.here.x] + self.x_rx[...]
+        self.full[self.here.z, self.here.x] = total
+        self.third.start()
+        self.square[...] = jnp.broadcast_to(total_square(total), self.square.shape)
+
+    def spread(self):
+        self.third.wait_recv()
+        begin(self.fourth)
+
+    def finish(self):
+        arrived(self.fourth)
 
 
 def total_square(v):
@@ -1025,6 +1066,8 @@
     part,
     x_rx,
     z_rx,
+    zz_rx,
+    xx_rx,
     core_rx,
     row_rx,
     gbc,
@@ -1061,13 +1104,15 @@
     thirds = chans // 128
     z_ref, x_ref, bc_ref, pre_ref = pieces(proj, chans, state)
     met = greet(group + far)
-    jobs = [
-        Piece(
-            here, links, part.at[i if i < 2 * thirds else i - thirds], x_rx.at[i], z_rx.at[i],
-            gfull.at[i], square_s.at[i],
-        )
-        for i in range(3 * thirds)
-    ]
+    jobs = []
+    crossing = (2 * thirds - 1, 2 * thirds)
+    for i in range(3 * thirds):
+        source = part.at[i if i < 2 * thirds else i - thirds]
+        k = sum(1 for other in crossing if other < i)
+        if i in crossing:
+            jobs.append(CrossPiece(here, links, source, zz_rx.at[k], xx_rx.at[k], gfull.at[i], square_s.at[i]))
+        else:
+            jobs.append(Piece(here, links, source, x_rx.at[i - k], z_rx.at[i - k], gfull.at[i], square_s.at[i]))
     z_jobs, x_jobs, o_jobs = jobs[0:thirds], jobs[thirds : 2 * thirds], jobs[2 * thirds :]
 
     half = bcw_ref.shape[0] // 2
@@ -1118,11 +1163,29 @@
         def wait(self):
             arrived(self.passed)
 
+    split = chans - 128
+
+    class Cross:
+        def __init__(self, ref):
+            self.mine, self.pair = ref.at[z, x, :, split:], ref.at[z, :, :, split:]
+
+        def begin(self):
+            self.across = links.copy(self.mine, self.mine, here.across)
+
+        def forward(self):
+            self.across.wait_recv()
+            self.sent = along(self.pair)
+
+        def wait(self):
+            arrived(self.sent)
+
     h_copies = exchange(hq.at[n])
     gain_copies = [links.copy(gain_g.at[n], gain_g.at[n], device) for device in group]
     early = Relay(lambda i: bc_g.at[i, x, c], lambda i: dt_g.at[i, x])
     early.begin()
-    first = Relay(lambda i: wx_g.at[i, x])
+    first_cross, second_cross, third_cross = Cross(wx_g), Cross(wz_g), Cross(wo_g)
+    first_cross.begin()
+    first = Relay(lambda i: wx_g.at[i, x, :, 0:split])
     first.begin()
 
     wz_g[z, x] = w_ref[0]
@@ -1156,9 +1219,11 @@
     cut(n)
     h_copies[1].wait_recv()
     cut(here.core[1])
+    first_cross.forward()
     early.forward()
     first.forward()
-    second = Relay(lambda i: wz_g.at[i, x])
+    second_cross.begin()
+    second = Relay(lambda i: wz_g.at[i, x, :, 0:split])
     h_copies[0].wait_recv()
     other = here.row[1]
     h_far = links.copy(hq.at[other], hq.at[other], here.core)
@@ -1210,8 +1275,10 @@
     bc_core_copy.wait_recv()
     turn(bc_g, 2 * chans)
     first.wait()
+    first_cross.wait()
     second.begin()
     second.forward((1,))
+    second_cross.forward()
     turn(wx_g, chans)
     second.forward((2,))
     h_far.wait_recv()
@@ -1219,7 +1286,8 @@
     cut(here.corner[1])
     project(proj.at[chans:], lambda: rows_of(chans, last + 16))
     second.forward((3,))
-    third = Relay(lambda i: wo_g.at[i, x])
+    third_cross.begin()
+    third = Relay(lambda i: wo_g.at[i, x, :, 0:split])
     third.begin()
     c_copies[0].wait_recv()
     c_far = links.copy(cq.at[other], cq.at[other], here.core)
@@ -1227,9 +1295,11 @@
     step_sizes(pre_ref, hp_ref, step_s, cum_s, cumex_s, heads)
     states(xc, b_s, step_s, cum_s, dh_s, hcat, heads)
     second.wait()
+    second_cross.wait()
     turn(wz_g, 0)
     project(z_ref, lambda: rows_of(0, chans))
     third.forward()
+    third_cross.forward()
 
     def stat_copy(j, b):
         return pltpu.make_async_remote_copy(
@@ -1309,6 +1379,7 @@
         for job in o_jobs[start:stop]:
             job.start()
     third.wait()
+    third_cross.wait()
     turn(wo_g, 0, False)
 
     def donorm(q):
@@ -1374,33 +1445,35 @@
     z0, z1, z2 = z_jobs
     x0, x1, x2 = x_jobs
     branch = Return(core_rx.at[0], row_rx.at[0], lambda q: dot3(flat(wo_g[...]), onorm[:, quarter(q)]))
-    o0.fold()
     told_inner = jnp.concatenate([told(blocks + b) for b in range(blocks)], axis=1)
     coef = rms**3 * told_inner / inner_total
     gate_back(z_ref, y_s, don, rms, coef, og_ref, dy_s, z_ref, dog_s)
+    o0.fold()
+    o1.fold()
     weight_grad(add_to(0, thirds), lambda q: z_ref[:, quarter(q)])
     for i, job in enumerate(z_jobs):
         scaled(i)
         job.start()
-    o1.fold()
-    o0.own()
 
     def x_grad(i):
-        links.release([o_jobs[i].first])
+        links.release(o_jobs[i].holding)
         part[thirds + i] = jnp.zeros(block_shape, F32)
         weight_grad(add_to(thirds + i, 1), lambda q: x_ref[i * 128 : (i + 1) * 128, quarter(q)])
         scaled(thirds + i)
 
     within = [
-        {0: [o2.fold], 6: [o1.own, z0.fold]},
-        {1: [o2.own, z2.fold], 3: [branch.fold], 5: [o1.spread]},
-        {0: [z1.own], 5: [o2.spread], 6: [x1.fold]},
+        {3: [o2.fold, o1.own], 5: [o0.own]},
+        {1: [o1.spread], 3: [branch.fold], 5: [o2.spread, z1.fold]},
+        {5: [z0.spread]},
     ]
-    between = [
-        {6: [o0.spread], 7: [z1.fold]},
-        {6: [z0.own, x0.fold]},
-        {4: [z2.own]},
-    ]
+    between = [{7: [o2.own]}, {3: [z0.own]}, {}]
+    after_states = [(), (), (x0.fold, z2.own)]
+    after_conv = [(z0.fold,), (), ()]
+    after_grad = [(), (z2.fold, z1.own, o0.spread), (z1.spread,)]
+
+    def run(steps):
+        for step in steps:
+            step()
 
     def ticks(plan):
         def tick(b):
@@ -1419,15 +1492,17 @@
             din_s, g_s, cv_s, dd_s, chosen, heads, ticks(within[i]),
         )
         back_states(cum_s, hcat, dh_s, tq_s, state, chosen, heads)
+        run(after_states[i])
         back_inter(xc, b_s, step_s, cum_s, y_s, dh_s, db_s, v_s, chosen, heads, ticks(between[i]))
         conv_x_back(x_ref, cx_ref, dx_act, y_s, x_ref, cols_s, i * 128, 128)
+        run(after_conv[i])
         x_grad(i)
         x_jobs[i].start()
+        run(after_grad[i])
 
     back_logs(
         b_s, c_s, pre_ref, step_s, hp_ref, pre_ref, dhp_s, db_s, dc_s, din_s, g_s, cv_s, v_s, dd_s, tq_s, heads
     )
-    z0.spread()
     conv_bc_back(bc_ref, cbc_ref, dbc_act, db_s, dc_s, bc_ref, dcbc_s)
     gbc_shape = gbc.shape
 
@@ -1438,8 +1513,6 @@
     weight_grad(add_bc, lambda q: bc_ref[:, quarter(q)])
     gbc[...] = (flat(gbc[...]) * gain_col[...]).reshape(gbc_shape)
     bc_first = links.copy(gbc.at[:, :, 1 - c], bc_core, here.core)
-    x0.own()
-    x2.fold()
     dt_grad = jnp.zeros((16, width), F32)
     for q in range(parts):
         step = halves(pre_ref[:, q * own_rows : (q + 1) * own_rows])
@@ -1479,7 +1552,7 @@
         dgain_s[...] = dgain_s[...] + jnp.sum(value * hq[q], axis=1, keepdims=True)
         return value
 
-    back = Return(core_rx.at[1], row_rx.at[1], normed_back, ([z1.spread], [], [x1.own], []))
+    back = Return(core_rx.at[1], row_rx.at[1], normed_back, ([], [x0.own], [], [x1.fold, z2.spread]))
     back.fold()
     small = 128
     shared_g[n] = jnp.zeros(shared_g.shape[1:], F32)
@@ -1501,7 +1574,7 @@
         sv_g[w, 0:4, sl] = jnp.transpose(cols_s[sl, :])[0:4]
         sv_g[w, 4:5, sl] = as_row(dog_s[sl, :])
     sv_g[w, :, chans : chans + small] = dhp_s[...]
-    z2.spread()
+    x2.fold()
     arrived(shared_copies)
     total = shared_g[0]
     for q in range(1, parts):
@@ -1509,6 +1582,8 @@
     sv_g[w, :, chans + small :] = total
     sv_copies = [links.copy(sv_g.at[w], sv_g.at[w], device) for device in far]
 
+    x0.spread()
+    x1.own()
     arrived(bc_copies)
     own = bc_rx[0]
     for k in range(1, wide):
@@ -1527,7 +1602,6 @@
     for k in range(1, wide):
         own = own + sv_g[k]
     sv_sum[...] = own
-    x0.spread()
     x2.own()
     for i in range(3 * thirds):
         squares = squares + square_s[i][:, 0:1]
@@ -1643,8 +1717,10 @@
         (2 * blocks, 8, 128),
         (narrow, 2 * blocks, 8, 128),
         (2 * thirds,) + piece[1:],
-        (3 * thirds, depth, rows, 128),
-        (3 * thirds, depth - 1, rows, 128),
+        (3 * thirds - 2, depth, rows, 128),
+        (3 * thirds - 2, depth - 1, rows, 128),
+        (2, depth - 1, 2, rows, 128),
+        (2, rows, 128),
         (2, 2, width, own_rows),
         (2, width, own_rows),
         (wide, 2, 2) + quarter,

time: 229 us -> 228 us (level); the launches traced: 227 us -> 228 us
  no operation moved by 1% of the time
where the time goes in v5:
time: 228 us
  Pallas kernels  227 us (100%)
    pallas_call x1, Pallas kernels, run_layer(): pl.pallas_call(functools.partial(layer_kernel, wide, heads, shard, chans...  215 us
    pallas_call x1, Pallas kernels, run_finish(): pl.pallas_call(functools.partial(finish_kernel, wide, narrow), out_shape=...  11.7 us

profile of v5, /device:TPU:0, one launch (start us, length us, event | category | flops | bytes accessed | tf_op | source)
XLA Modules:
  0.0 228.2 jit_solution(11079343135387264130)
XLA Ops:
  1.3 215.0 %shard_map.387 = (f32[256,768]{1,0:T(8,128)}, f32[256,768]{1,0:T(8,128)}, f32[9,4,2,96,128]{4,3,2,1,0:T(8,128)}, f32[4,24,256]{2,1,0:T(8,128)}, f32[16,128]{1,0:...) custom-call(s32[1]{0:T(128)S(6)} %copy.46.length_ref, f32[256,768]{1,0:T(8,128)} %hidden_ref.1, f32[256,768]{1,0:T(8,128)} %cot_ref.1, ...), custom_call_target="tpu_custom_call" | custom-call | flops 20000000000 | bytes 20000000 | tf_op jit(solution)/shard_map/pallas_call | solution.py:1742
  216.3 11.7 %shard_map.388 = (f32[256,768]{1,0:T(8,128)}, f32[256,768]{1,0:T(8,128)}, f32[1,1]{1,0:T(1,128)}, f32[2,96,384]{2,1,0:T(8,128)}, f32[2,96,384]{2,1,0:T(8,128)}, ...) custom-call(f32[9,4,2,96,128]{4,3,2,1,0:T(8,128)} %get-tuple-element, ...), custom_call_target="tpu_custom_call" | custom-call | flops 4000000000 | bytes 20000000 | tf_op jit(solution)/shard_map/pallas_call | solution.py:1933

commit v6 on v5

--- a/solution.py
+++ b/solution.py
@@ -1401,24 +1401,28 @@
     class Return:
         def __init__(self, rx, row_rx, compute, steps=((), (), (), ())):
             self.rx, self.row_rx = rx, row_rx
-            first = links.count
-            self.cores = [links.plan(cq.at[k * 2 + 1 - c], rx.at[k], here.core) for k in range(2)]
-            self.last = links.plan(rx.at[1 - y], row_rx, here.row)
+            near, away = y * 2, (1 - y) * 2
+            self.cores = [
+                links.plan(cq.at[away + 1 - c], rx.at[0], here.core),
+                links.plan(cq.at[near + 1 - c], rx.at[1], here.core),
+            ]
+            self.last = links.plan(cq.at[away + c], row_rx, here.row)
 
             def body(k, _):
-                q = (k % 2) * 2 + (c + 1 + k // 2) % 2
+                row = 1 - y + (k // 2) * (2 * y - 1)
+                q = row * 2 + 1 - c + (k % 2) * (2 * c - 1)
                 cq[q] = compute(q)
 
-                @pl.when(k < 2)
+                @pl.when(k == 0)
                 def _():
-                    pltpu.make_async_remote_copy(
-                        src_ref=cq.at[q],
-                        dst_ref=rx.at[k % 2],
-                        send_sem=links.send.at[first + k % 2],
-                        recv_sem=links.recv.at[first + k % 2],
-                        device_id=here.core,
-                        device_id_type=MESH,
-                    ).start()
+                    self.cores[0].start()
+
+                @pl.when(k == 2)
+                def _():
+                    self.cores[1].start()
+                    self.cores[0].wait_recv()
+                    cq[away + c] = cq[away + c] + rx[0]
+                    self.last.start()
 
                 for at, items in enumerate(steps):
 
@@ -1432,14 +1436,12 @@
             lax.fori_loop(0, 4, body, 0)
 
         def fold(self):
-            arrived(self.cores)
-            for k in range(2):
-                self.rx[k] = self.rx[k] + cq[k * 2 + c]
-            self.last.start()
+            self.cores[1].wait_recv()
+            self.rx[1] = self.rx[1] + cq[y * 2 + c]
 
         def total(self):
             self.last.wait_recv()
-            return self.rx[y] + self.row_rx[...]
+            return self.rx[1] + self.row_rx[...]
 
     o0, o1, o2 = o_jobs
     z0, z1, z2 = z_jobs
@@ -1531,7 +1533,7 @@
         bc_mine[k] = bc_core[k, 1 - y]
     bc_second = links.copy(bc_mine, bc_row, here.row)
 
-    links.release(branch.cores)
+    links.release(branch.cores + [branch.last])
 
     for k in range(parts):
         pieces_of = []
@@ -1861,21 +1863,23 @@
             item.wait()
         parts = [flat(g_s[m * thirds + i]) for i in range(thirds)]
         mine = [g_s[m * thirds + i, z, x] for i in range(thirds)]
-        return jnp.concatenate(mine, axis=1) * factor, halves(jnp.concatenate(parts, axis=1) * factor)
-
-    own, full = both(2)
+        parts = [item * factor for item in parts]
+        turned = jnp.concatenate([jnp.transpose(item) for item in parts], axis=0)
+        return jnp.concatenate(mine, axis=1) * factor, halves(jnp.concatenate(parts, axis=1)), halves(turned)
+
+    own, full, turned = both(2)
     g_out[...] = own
     ro_s[...] = 0.5 * ro_s[...] + 0.5 * product(halves(own), full, NT)
     result(ro_s, new_ro)
-    lo_s[...] = 0.5 * lo_s[...] + 0.5 * product(full, full, TN)
+    lo_s[...] = 0.5 * lo_s[...] + 0.5 * product(turned, full)
     result(lo_s, new_lo)
     new_out[...] = wout_ref[...] - 0.5 * dot3(product(halves(rro_s[...]), full), rlo_s[...], NT)
     for m in range(2):
-        own, full = both(m)
+        own, full, turned = both(m)
         g_zx[m] = own
         l_s[m] = 0.5 * l_s[m] + 0.5 * product(halves(own), full, NT)
         result(l_s.at[m], new_l.at[m])
-        r_s[m] = 0.5 * r_s[m] + 0.5 * product(full, full, TN)
+        r_s[m] = 0.5 * r_s[m] + 0.5 * product(turned, full)
         result(r_s.at[m], new_r.at[m])
         new_zx[m] = w_ref[m] - 0.5 * dot3(product(halves(rl_s[m]), full), rr_s[m])
 

time: 228 us -> 226 us (level)
  Pallas kernels: 227 us -> 223 us
    pallas_call x1, Pallas kernels: 215 us -> 211 us  [run_layer(): pl.pallas_call(functools.partial(layer_kernel, wide, heads, shard, chans...]
where the time goes in v6:
time: 226 us; the launch traced here: 225 us
  Pallas kernels  223 us (99%)
    pallas_call x1, Pallas kernels, run_layer(): pl.pallas_call(functools.partial(layer_kernel, wide, heads, shard, chans...  211 us
    pallas_call x1, Pallas kernels, run_finish(): pl.pallas_call(functools.partial(finish_kernel, wide, narrow), out_shape=...  11.6 us

profile of v6, /device:TPU:0, one launch (start us, length us, event | category | flops | bytes accessed | tf_op | source)
XLA Modules:
  0.0 224.5 jit_solution(8057976306048923094)
XLA Ops:
  1.3 211.3 %shard_map.387 = (f32[256,768]{1,0:T(8,128)}, f32[256,768]{1,0:T(8,128)}, f32[9,4,2,96,128]{4,3,2,1,0:T(8,128)}, f32[4,24,256]{2,1,0:T(8,128)}, f32[16,128]{1,0:...) custom-call(s32[1]{0:T(128)S(6)} %copy.46.length_ref, f32[256,768]{1,0:T(8,128)} %hidden_ref.1, f32[256,768]{1,0:T(8,128)} %cot_ref.1, ...), custom_call_target="tpu_custom_call" | custom-call | flops 20000000000 | bytes 20000000 | tf_op jit(solution)/shard_map/pallas_call | solution.py:1744
  212.7 11.6 %shard_map.388 = (f32[256,768]{1,0:T(8,128)}, f32[256,768]{1,0:T(8,128)}, f32[1,1]{1,0:T(1,128)}, f32[2,96,384]{2,1,0:T(8,128)}, f32[2,96,384]{2,1,0:T(8,128)}, ...) custom-call(f32[9,4,2,96,128]{4,3,2,1,0:T(8,128)} %get-tuple-element, ...), custom_call_target="tpu_custom_call" | custom-call | flops 4000000000 | bytes 20000000 | tf_op jit(solution)/shard_map/pallas_call | solution.py:1937

commit v7 on v6

--- a/solution.py
+++ b/solution.py
@@ -1079,6 +1079,7 @@
     dt_rx,
     shared_g,
     sv_g,
+    sw_g,
     norm_n,
     norm_w,
     square_s,
@@ -1505,7 +1506,17 @@
     back_logs(
         b_s, c_s, pre_ref, step_s, hp_ref, pre_ref, dhp_s, db_s, dc_s, din_s, g_s, cv_s, v_s, dd_s, tq_s, heads
     )
+    x0.own()
     conv_bc_back(bc_ref, cbc_ref, dbc_act, db_s, dc_s, bc_ref, dcbc_s)
+    x1.fold()
+    small = 128
+    sv_g[w] = jnp.zeros(sv_g.shape[1:], F32)
+    for i in range(thirds):
+        sl = slice(i * 128, (i + 1) * 128)
+        sv_g[w, 0:4, sl] = jnp.transpose(cols_s[sl, :])[0:4]
+        sv_g[w, 4:5, sl] = as_row(dog_s[sl, :])
+    sv_g[w, :, chans : chans + small] = dhp_s[...]
+    sv_copies = [links.copy(sv_g.at[w], sv_g.at[w], device) for device in far]
     gbc_shape = gbc.shape
 
     def add_bc(q, value):
@@ -1515,6 +1526,8 @@
     weight_grad(add_bc, lambda q: bc_ref[:, quarter(q)])
     gbc[...] = (flat(gbc[...]) * gain_col[...]).reshape(gbc_shape)
     bc_first = links.copy(gbc.at[:, :, 1 - c], bc_core, here.core)
+    x2.fold()
+    z2.spread()
     dt_grad = jnp.zeros((16, width), F32)
     for q in range(parts):
         step = halves(pre_ref[:, q * own_rows : (q + 1) * own_rows])
@@ -1525,6 +1538,7 @@
         gdt[i, :, 0:lanes] = dt_grad[:, i * lanes : (i + 1) * lanes]
     dt_rx[w] = gdt[w]
     dt_copies = [links.copy(gdt.at[device[0]], dt_rx.at[w], device) for device in far]
+    x0.spread()
     dgain_s[...] = jnp.zeros_like(dgain_s)
     bc_first.wait_recv()
     for k in range(2):
@@ -1554,9 +1568,7 @@
         dgain_s[...] = dgain_s[...] + jnp.sum(value * hq[q], axis=1, keepdims=True)
         return value
 
-    back = Return(core_rx.at[1], row_rx.at[1], normed_back, ([], [x0.own], [], [x1.fold, z2.spread]))
-    back.fold()
-    small = 128
+    back = Return(core_rx.at[1], row_rx.at[1], normed_back, ([x1.own], [x2.own], [x1.spread], [x2.spread]))
     shared_g[n] = jnp.zeros(shared_g.shape[1:], F32)
     for i in range(4 * state // 128):
         sl = slice(i * 128, (i + 1) * 128)
@@ -1570,50 +1582,36 @@
         bc_mine[k] = bc_core[k, y] + bc_row[k]
     bc_rx[w] = bc_mine[w]
     bc_copies = [links.copy(bc_mine.at[device[0]], bc_rx.at[w], device) for device in far]
-    sv_g[w] = jnp.zeros(sv_g.shape[1:], F32)
-    for i in range(thirds):
-        sl = slice(i * 128, (i + 1) * 128)
-        sv_g[w, 0:4, sl] = jnp.transpose(cols_s[sl, :])[0:4]
-        sv_g[w, 4:5, sl] = as_row(dog_s[sl, :])
-    sv_g[w, :, chans : chans + small] = dhp_s[...]
-    x2.fold()
+    back.fold()
+    arrived(dt_copies)
+    own = dt_rx[0]
+    for k in range(1, wide):
+        own = own + dt_rx[k]
+    dt_own[...] = own
+    squares = total_square(own)
+    arrived(sv_copies)
+    own = sv_g[0]
+    for k in range(1, wide):
+        own = own + sv_g[k]
+    sv_sum[:, 0 : chans + small] = own
+    squares = squares + jnp.where(w == 0, 1.0, 0.0) * total_square(own)
+    for i in range(3 * thirds):
+        squares = squares + square_s[i][:, 0:1]
     arrived(shared_copies)
     total = shared_g[0]
     for q in range(1, parts):
         total = total + shared_g[q]
-    sv_g[w, :, chans + small :] = total
-    sv_copies = [links.copy(sv_g.at[w], sv_g.at[w], device) for device in far]
-
-    x0.spread()
-    x1.own()
+    sw_g[w] = total
+    sw_copies = [links.copy(sw_g.at[w], sw_g.at[w], device) for device in far]
     arrived(bc_copies)
     own = bc_rx[0]
     for k in range(1, wide):
         own = own + bc_rx[k]
     bc_own[n] = own
     bc_group = [links.copy(bc_own.at[n], bc_own.at[n], device) for device in group]
-    squares = total_square(own)
-    arrived(dt_copies)
-    own = dt_rx[0]
-    for k in range(1, wide):
-        own = own + dt_rx[k]
-    dt_own[...] = own
     squares = squares + total_square(own)
-    arrived(sv_copies)
-    own = sv_g[0]
-    for k in range(1, wide):
-        own = own + sv_g[k]
-    sv_sum[...] = own
-    x2.own()
-    for i in range(3 * thirds):
-        squares = squares + square_s[i][:, 0:1]
-    once = jnp.where(w == 0, 1.0, 0.0)
-    squares = squares + once * total_square(own[:, 0 : chans + small])
-    squares = squares + jnp.where(n == 0, once, 0.0) * total_square(own[:, chans + small :])
     norm_n[n] = jnp.broadcast_to(squares, (8, 128))
     norm_copies = [links.copy(norm_n.at[n], norm_n.at[n], device) for device in group]
-
-    x1.spread()
 
     block = branch.total() * live_ref[:, pl.ds(pl.multiple_of(n * own_rows, 128), own_rows)]
     for i in range(width // 128):
@@ -1622,17 +1620,22 @@
     arrived(norm_copies)
     norm_w[w] = norm_n[0] + norm_n[1] + norm_n[2] + norm_n[3]
     wide_copies = [links.copy(norm_w.at[w], norm_w.at[w], device) for device in far]
-    x2.spread()
     dn = back.total() * gain_col[...]
     dots = jnp.sum(dn * hq[n], axis=0, keepdims=True) / width
     for i in range(width // 128):
         sl = slice(i * 128, (i + 1) * 128)
         value = inv_ref[...] * (dn[sl] - hq[n, sl, :] * dots)
         grad_ref[:, sl] = cot_ref[:, sl] + jnp.transpose(value)
+    arrived(sw_copies)
+    shared = sw_g[0]
+    for k in range(1, wide):
+        shared = shared + sw_g[k]
+    sv_sum[:, chans + small :] = shared
     arrived(wide_copies)
     total = norm_w[0]
     for k in range(1, wide):
         total = total + norm_w[k]
+    total = total + total_square(shared)
     norm_ref[...] = jnp.sqrt(total)
     for job in jobs:
         job.finish()
@@ -1733,7 +1736,8 @@
         (wide, 16, 128),
         (wide, 16, 128),
         (narrow, 16, 256),
-        (wide,) + sums,
+        (wide, 16, chans + 128),
+        (wide, 16, 256),
         (narrow, 8, 128),
         (wide, 8, 128),
         (3 * thirds, 1, 128),

time: 226 us -> 225 us (level)
  no operation moved by 1% of the time
where the time goes in v7:
time: 225 us; the launch traced here: 224 us
  Pallas kernels  223 us (99%)
    pallas_call x1, Pallas kernels, run_layer(): pl.pallas_call(functools.partial(layer_kernel, wide, heads, shard, chans...  211 us
    pallas_call x1, Pallas kernels, run_finish(): pl.pallas_call(functools.partial(finish_kernel, wide, narrow), out_shape=...  11.6 us

profile of v7, /device:TPU:0, one launch (start us, length us, event | category | flops | bytes accessed | tf_op | source)
XLA Modules:
  0.0 224.5 jit_solution(14941010158741983865)
XLA Ops:
  1.3 211.3 %shard_map.387 = (f32[256,768]{1,0:T(8,128)}, f32[256,768]{1,0:T(8,128)}, f32[9,4,2,96,128]{4,3,2,1,0:T(8,128)}, f32[4,24,256]{2,1,0:T(8,128)}, f32[16,128]{1,0:...) custom-call(s32[1]{0:T(128)S(6)} %copy.46.length_ref, f32[256,768]{1,0:T(8,128)} %hidden_ref.1, f32[256,768]{1,0:T(8,128)} %cot_ref.1, ...), custom_call_target="tpu_custom_call" | custom-call | flops 20000000000 | bytes 20000000 | tf_op jit(solution)/shard_map/pallas_call | solution.py:1748
  212.6 11.6 %shard_map.388 = (f32[256,768]{1,0:T(8,128)}, f32[256,768]{1,0:T(8,128)}, f32[1,1]{1,0:T(1,128)}, f32[2,96,384]{2,1,0:T(8,128)}, f32[2,96,384]{2,1,0:T(8,128)}, ...) custom-call(f32[9,4,2,96,128]{4,3,2,1,0:T(8,128)} %get-tuple-element, ...), custom_call_target="tpu_custom_call" | custom-call | flops 4000000000 | bytes 20000000 | tf_op jit(solution)/shard_map/pallas_call | solution.py:1941
